TPU v7x, 256 devices: a whole 4x4x8 slice. The times are simulated.
256 devices in a mesh: tm: 8 (over x_hi, y), space: 32 (over x_lo, z, core).
Axes of the slice: x: 4 (x_hi: 2, x_lo: 2; x = x_hi * 2 + x_lo), y: 4, z: 8, core: 2. Of those that a mesh axis runs over, the one named last changes fastest.
Arguments:
- node_values: float32 [8, 3, 8, 512, 2048], P('tm', None, None, 'space'), may hold values from -1 to 1
Outputs:
- next_iterate: float32 [8, 3, 8, 512, 2048], P('tm', None, None, 'space')
All inputs are finite; a program needn't handle non-finite values.
Results may differ from a plain program's by a relative error of at most 0.0001.
Values sent between devices are 32-bit elements; how exact they have to be, the bound alone decides.
A program may use at most 64 MiB of HBM per device.

v0:
```python
import functools

import jax
import jax.numpy as jnp
from jax import lax
from jax.experimental import pallas as pl
from jax.experimental.pallas import tpu as pltpu
from jax.sharding import PartitionSpec as P

STEP = 0.25
WEIGHTS = ((5.0 / 24.0, 1.0 / 3.0, -1.0 / 24.0), (-1.0 / 24.0, 1.0 / 3.0, 5.0 / 24.0))
MESH = pl.DeviceIdType.MESH
F32 = jnp.float32


def fine_rate(above, center, below):
    lanes = center.shape[-1]
    beside = above + below + pltpu.roll(center, 1, 0) + pltpu.roll(center, 7, 0)
    beside = beside + pltpu.roll(center, 1, 1) + pltpu.roll(center, lanes - 1, 1)
    return beside - center * (4.0 + 2.0 * (center * center))


def iotas():
    sub = lax.broadcasted_iota(jnp.int32, (8, 128), 0)
    lane = lax.broadcasted_iota(jnp.int32, (8, 128), 1)
    return sub, lane


def take(value, index, axis):
    return jnp.take_along_axis(value, index, axis=axis, mode="promise_in_bounds")


def split_tiles(value):
    return [value[:, 128 * t : 128 * (t + 1)] for t in range(value.shape[1] // 128)]


def lane_neighbours(tiles, lane):
    count = len(tiles)
    right_rolled = [pltpu.roll(t, 1, 1) for t in tiles]
    left_rolled = [pltpu.roll(t, 127, 1) for t in tiles]
    before = [pltpu.roll(right_rolled[-1], 4, 0)] + right_rolled[:-1]
    after = left_rolled[1:] + [pltpu.roll(left_rolled[0], 4, 0)]
    left = [jnp.where(lane == 0, before[i], right_rolled[i]) for i in range(count)]
    right = [jnp.where(lane == 127, after[i], left_rolled[i]) for i in range(count)]
    return left, right


def coarse_rate(above, center, below):
    sub, lane = iotas()
    up_index = (sub // 4) * 4 + (sub + 1) % 4
    down_index = (sub // 4) * 4 + (sub + 3) % 4
    a, c, b = split_tiles(above), split_tiles(center), split_tiles(below)
    left, right = lane_neighbours(c, lane)
    out = []
    for i in range(len(c)):
        beside = a[i] + b[i] + take(c[i], up_index, 0) + take(c[i], down_index, 0) + left[i] + right[i]
        out.append(0.25 * beside + c[i] * (0.5 - 2.0 * (c[i] * c[i])))
    return jnp.concatenate(out, axis=1)


def restrict_row(pair_sum, staging):
    sub, lane = iotas()
    tiles = split_tiles(pair_sum)
    half = len(tiles) // 2
    for t in range(half):
        staging[pl.ds(16 * t, 8), :] = tiles[t]
        staging[pl.ds(16 * t + 8, 8), :] = tiles[t + half]
    packed = [
        staging[pl.ds(16 * t, 8, stride=2), :] + staging[pl.ds(16 * t + 1, 8, stride=2), :]
        for t in range(half)
    ]
    index = jnp.where(lane < 64, 2 * lane, 2 * lane - 127)
    out = []
    for t in range(half // 2):
        p, q = packed[2 * t], packed[2 * t + 1]
        mixed = jnp.where(lane % 2 == 0, p + pltpu.roll(p, 127, 1), q + pltpu.roll(q, 1, 1))
        out.append(0.125 * take(mixed, index, 1))
    return jnp.concatenate(out, axis=1)


def main_kernel(
    u_hbm, vv_hbm, d_hbm,
    ub, v1, tt, f0, v2, g1, c0, c1, c2, c2p, a0, a1, w0, w1, w2, dd, staging,
    load_sem, u_send, u_recv, h_send, h_recv, w_send, w_recv, v_send, v_recv, p_send, p_recv, out_sem,
):
    tm, sp = lax.axis_index("tm"), lax.axis_index("space")
    n_tm, n_sp = lax.axis_size("tm"), lax.axis_size("space")
    left, right = lax.rem(sp + n_sp - 1, n_sp), lax.rem(sp + 1, n_sp)
    not_first, not_last = tm > 0, tm < n_tm - 1
    half_step = 0.5 * STEP

    def load(m, r):
        return pltpu.make_async_copy(u_hbm.at[0, m, :, r, :], ub.at[m, r + 3], load_sem.at[m, r])

    def remote(src, dst, send, recv, t, s):
        return pltpu.make_async_remote_copy(
            src_ref=src, dst_ref=dst, send_sem=send, recv_sem=recv, device_id=(t, s), device_id_type=MESH
        )

    def edge_row(k):
        return jnp.where(k < 3, k, k + 10)

    def each(count, body):
        def step(k, carry):
            body(k)
            return carry

        lax.fori_loop(0, count, step, 0)

    def load_edges(k):
        for m in range(3):
            load(m, edge_row(k)).start()

    def load_inner(k):
        for m in range(3):
            load(m, k + 3).start()

    each(6, load_edges)
    each(10, load_inner)

    barrier = pltpu.get_barrier_semaphore()
    for s in (left, right):
        pl.semaphore_signal(barrier, inc=1, device_id=(tm, s), device_id_type=MESH)

    @pl.when(not_first)
    def _():
        for s in (left, sp, right):
            pl.semaphore_signal(barrier, inc=1, device_id=(tm - 1, s), device_id_type=MESH)

    @pl.when(not_last)
    def _():
        pl.semaphore_wait(barrier, 5)

    @pl.when(jnp.logical_not(not_last))
    def _():
        pl.semaphore_wait(barrier, 2)

    def wait_edges(k):
        for m in range(3):
            load(m, edge_row(k)).wait()

    def wait_inner(k):
        for m in range(3):
            load(m, k + 3).wait()

    each(6, wait_edges)
    u_up = remote(ub.at[:, pl.ds(16, 3)], ub.at[:, pl.ds(0, 3)], u_send.at[0], u_recv.at[0], tm, right)
    u_down = remote(ub.at[:, pl.ds(3, 3)], ub.at[:, pl.ds(19, 3)], u_send.at[1], u_recv.at[1], tm, left)
    u_up.start()
    u_down.start()
    each(10, wait_inner)

    def first_sweep(r):
        rates = [fine_rate(ub[m, r + 2], ub[m, r + 3], ub[m, r + 4]) for m in range(3)]
        (a, b, c), (d, e, f) = WEIGHTS
        v1[r + 2] = ub[0, r + 3] + (STEP * a) * rates[0] + (STEP * b) * rates[1] + (STEP * c) * rates[2]
        return rates, (STEP * d) * rates[0] + (STEP * e - half_step) * rates[1] + (STEP * f) * rates[2]

    def first_sweep_inner(r):
        rates, rest = first_sweep(r)
        f0[r] = rates[0]
        tt[r + 1] = rest

    def second_sweep(r):
        rate = fine_rate(v1[r + 1], v1[r + 2], v1[r + 3])
        v2[r + 1] = v1[r + 2] + half_step * rate + tt[r + 1]
        return rate

    def second_sweep_inner(r):
        g1[r] = second_sweep(r)

    def restrict_start(i):
        c0[i + 1] = restrict_row(ub[0, 2 * i + 3] + ub[0, 2 * i + 4], staging.at[0])
        c1[i + 1] = restrict_row(v1[2 * i + 2] + v1[2 * i + 3], staging.at[1])

    def third_sweep(i):
        r = 2 * i
        (a, b, c), (d, e, f) = WEIGHTS
        sums = [0.0, 0.0]
        for k in range(2):
            g2 = fine_rate(v2[r + k], v2[r + k + 1], v2[r + k + 2])
            sums[0] = sums[0] + (STEP * a) * f0[r + k] + (STEP * b) * g1[r + k] + (STEP * c) * g2
            sums[1] = sums[1] + (STEP * d) * f0[r + k] + (STEP * e) * g1[r + k] + (STEP * f) * g2
        a0[i + 2] = restrict_row(sums[0], staging.at[2])
        a1[i + 1] = restrict_row(sums[1], staging.at[3])
        c2[i + 1] = restrict_row(v2[r + 1] + v2[r + 2], staging.at[4])

    each(14, lambda k: first_sweep_inner(k + 1))
    each(12, lambda k: second_sweep_inner(k + 2))

    def inner_pairs(k):
        restrict_start(k + 2)
        third_sweep(k + 2)

    each(4, inner_pairs)

    u_up.wait_recv()
    u_down.wait_recv()

    def first_rim(k):
        first_sweep_inner(15 * k)

    def first_far(k):
        r = 17 * k - 1
        tt[r + 1] = first_sweep(r)[1]

    def first_farthest(k):
        first_sweep(19 * k - 2)

    each(2, first_rim)
    each(2, first_far)
    each(2, first_farthest)
    each(4, lambda k: second_sweep_inner(jnp.where(k < 2, k, k + 12)))
    each(2, lambda k: second_sweep(17 * k - 1))
    each(4, lambda k: third_sweep(jnp.where(k < 2, k, k + 4)))
    each(6, lambda k: restrict_start(jnp.where(k < 3, k - 1, k + 3)))

    def edge_sends(rows, t):
        up = remote(rows.at[pl.ds(5, 3)], w0.at[pl.ds(0, 3)], w_send.at[0], w_recv.at[0], t, right)
        down = remote(rows.at[pl.ds(0, 3)], w0.at[pl.ds(11, 3)], w_send.at[1], w_recv.at[1], t, left)
        return up, down

    own_c0, own_w2 = c0.at[pl.ds(1, 8)], w2.at[pl.ds(1, 8)]
    start_up, start_down = edge_sends(own_c0, tm)
    next_up, next_down = edge_sends(own_w2, tm + 1)
    next_own = remote(own_w2, w0.at[pl.ds(3, 8)], w_send.at[2], w_recv.at[2], tm + 1, sp)
    is_first = jnp.logical_not(not_first)

    @pl.when(is_first)
    def _():
        start_up.start()
        start_down.start()

    def halo_sends(index, field, rows, own):
        up = remote(field.at[pl.ds(own + 8 - rows, rows)], field.at[pl.ds(own - rows, rows)], h_send.at[index], h_recv.at[index], tm, right)
        down = remote(field.at[pl.ds(own, rows)], field.at[pl.ds(own + 8, rows)], h_send.at[index + 1], h_recv.at[index + 1], tm, left)
        return [up, down]

    c2_halos = halo_sends(0, c2, 1, 1)
    a_halos = halo_sends(2, a0, 2, 2) + halo_sends(4, a1, 1, 1)

    def add_start(k):
        a0[k + 2] = a0[k + 2] - half_step * coarse_rate(c0[k], c0[k + 1], c0[k + 2])
        a1[k + 1] = a1[k + 1] - half_step * coarse_rate(c1[k], c1[k + 1], c1[k + 2])

    each(8, add_start)
    for copy in a_halos + c2_halos:
        copy.start()

    v1_out = pltpu.make_async_copy(v1.at[pl.ds(2, 16)], vv_hbm.at[1], out_sem.at[0])
    v2_out = pltpu.make_async_copy(v2.at[pl.ds(1, 16)], vv_hbm.at[2], out_sem.at[1])
    u0_out = pltpu.make_async_copy(ub.at[0, pl.ds(3, 16)], vv_hbm.at[0], out_sem.at[2])
    v_next = remote(v2.at[pl.ds(1, 16)], vv_hbm.at[0], v_send.at[0], v_recv.at[0], tm + 1, sp)
    v1_out.start()
    v2_out.start()

    early = tm >= n_tm // 2

    @pl.when(is_first)
    def _():
        u0_out.start()
        w0[pl.ds(3, 8)] = c0[pl.ds(1, 8)]

    @pl.when(not_last & early)
    def _():
        v_next.start()

    for copy in a_halos + c2_halos:
        copy.wait_recv()
    p_next = remote(c2, c2p, p_send.at[0], p_recv.at[0], tm + 1, sp)

    @pl.when(not_last)
    def _():
        p_next.start()

    @pl.when(not_first)
    def _():
        next_own.wait_recv()

    start_up.wait_recv()
    start_down.wait_recv()

    def middle(k):
        w1[k] = w0[k + 1] + half_step * coarse_rate(w0[k], w0[k + 1], w0[k + 2]) + a0[k]

    def finish(k):
        w2[k] = w1[k + 1] + half_step * coarse_rate(w1[k], w1[k + 1], w1[k + 2]) + a1[k]

    each(12, middle)
    each(10, finish)

    @pl.when(not_last)
    def _():
        next_own.start()
        next_up.start()
        next_down.start()

    @pl.when(not_last & jnp.logical_not(early))
    def _():
        v_next.start()

    dd[1] = w1[pl.ds(1, 10)] - c1[...]
    dd[2] = w2[...] - c2[...]

    @pl.when(not_first)
    def _():
        p_next.wait_recv()
        dd[0] = w0[pl.ds(2, 10)] - c2p[...]

    @pl.when(is_first)
    def _():
        dd[0] = jnp.zeros(dd.shape[1:], F32)

    d_out = pltpu.make_async_copy(dd, d_hbm, out_sem.at[3])
    d_out.start()

    u_up.wait_send()
    u_down.wait_send()
    for copy in a_halos + c2_halos:
        copy.wait_send()

    @pl.when(is_first)
    def _():
        start_up.wait_send()
        start_down.wait_send()
        u0_out.wait()

    @pl.when(not_last)
    def _():
        next_own.wait_send()
        next_up.wait_send()
        next_down.wait_send()
        p_next.wait_send()
        v_next.wait_send()

    @pl.when(not_first)
    def _():
        v_next.wait_recv()

    v1_out.wait()
    v2_out.wait()
    d_out.wait()


def correct_kernel(vv_hbm, d_ref, o_hbm, vb, g75, g25, in_sem, out_sem):
    sub, lane = iotas()
    lanes = vb.shape[-1]
    half = lanes // 256

    def load(m):
        return pltpu.make_async_copy(vv_hbm.at[m], vb.at[m], in_sem.at[m])

    def store(m, r):
        return pltpu.make_async_copy(vb.at[m, r], o_hbm.at[0, m, :, r, :], out_sem.at[m, r])

    for m in range(3):
        load(m).start()

    def spread(m, k):
        tiles = split_tiles(d_ref[m, k])
        before, after = lane_neighbours(tiles, lane)
        for t in range(half):
            i, index = t // 2, (t % 2) * 64 + lane // 2
            low = 0.75 * tiles[i] + 0.25 * before[i]
            high = 0.75 * tiles[i] + 0.25 * after[i]
            fine = jnp.where(lane % 2 == 0, take(low, index, 1), take(high, index, 1))
            near_part, far_part = 0.75 * fine, 0.25 * fine
            for h in range(2):
                near = 4 * h + sub // 2
                far = 4 * h + (sub // 2 + 3 + 2 * (sub % 2)) % 4
                value = take(near_part, near, 0) + take(far_part, far, 0)
                columns = pl.ds(128 * (t + half * h), 128)
                g75[k, :, columns] = 0.75 * value
                g25[k, :, columns] = 0.25 * value

    def node(m, carry):
        def spread_step(k, inner):
            spread(m, k)
            return inner

        lax.fori_loop(0, 10, spread_step, 0)
        load(m).wait()

        def rows(k, inner):
            vb[m, 2 * k] = vb[m, 2 * k] + g75[k + 1] + g25[k]
            vb[m, 2 * k + 1] = vb[m, 2 * k + 1] + g75[k + 1] + g25[k + 2]
            store(m, 2 * k).start()
            store(m, 2 * k + 1).start()
            return inner

        lax.fori_loop(0, 8, rows, 0)
        return carry

    lax.fori_loop(0, 3, node, 0)

    def drain(k, carry):
        for m in range(3):
            store(m, k).wait()
        return carry

    lax.fori_loop(0, 16, drain, 0)


def on_device(node_values):
    _, _, depth, rows, lanes = node_values.shape
    half = lanes // 4
    fine = lambda n: pltpu.VMEM((n, 8, lanes), F32)
    coarse = lambda n: pltpu.VMEM((n, 8, half), F32)
    dma = lambda *n: pltpu.SemaphoreType.DMA(n)
    anywhere = pl.BlockSpec(memory_space=pl.ANY)
    vv, dd = pl.pallas_call(
        main_kernel,
        name="sweeps",
        out_shape=(
            jax.ShapeDtypeStruct((3, rows, depth, lanes), F32),
            jax.ShapeDtypeStruct((3, 10, 8, half), F32),
        ),
        in_specs=[anywhere],
        out_specs=(anywhere, anywhere),
        scratch_shapes=[
            pltpu.VMEM((3, 22, 8, lanes), F32), fine(20), fine(18), fine(16), fine(18), fine(16),
            coarse(10), coarse(10), coarse(10), coarse(10), coarse(12), coarse(10), coarse(14), coarse(12), coarse(10),
            pltpu.VMEM((3, 10, 8, half), F32), pltpu.VMEM((5, lanes // 16, 128), F32),
            dma(3, 16), dma(2), dma(2), dma(6), dma(6), dma(3), dma(3), dma(1), dma(1), dma(1), dma(1), dma(4),
        ],
        compiler_params=pltpu.CompilerParams(
            collective_id=0, has_side_effects=True, vmem_limit_bytes=48 * 1024 * 1024
        ),
    )(node_values)
    return pl.pallas_call(
        correct_kernel,
        name="correct",
        out_shape=jax.ShapeDtypeStruct(node_values.shape, F32),
        in_specs=[anywhere, pl.BlockSpec(memory_space=pltpu.VMEM)],
        out_specs=anywhere,
        scratch_shapes=[
            pltpu.VMEM((3, rows, 8, lanes), F32), pltpu.VMEM((10, 8, lanes), F32), pltpu.VMEM((10, 8, lanes), F32),
            dma(3), dma(3, 16),
        ],
        compiler_params=pltpu.CompilerParams(vmem_limit_bytes=48 * 1024 * 1024),
    )(vv, dd)


def solution(mesh):
    return jax.shard_map(
        on_device,
        mesh=mesh,
        in_specs=(P("tm", None, None, "space", None),),
        out_specs=P("tm", None, None, "space", None),
        check_vma=False,
    )
```

profile of v0, /device:TPU:31, one launch (start us, length us, event | category | flops | bytes accessed | tf_op | source)
XLA Modules:
  0.0 94.2 jit_solution(14245129691367914314)
XLA Ops:
  0.0 86.5 %sweeps.1 = (f32[3,16,8,2048]{3,2,1,0:T(8,128)S(1)}, f32[3,10,8,512]{3,2,1,0:T(8,128)S(1)}) custom-call(f32[1,3,8,16,2048]{4,3,2,1,0:T(8,128)} %u_hbm.1), custom_call_target="tpu_custom_call" | custom-call | tf_op jit(solution)/shard_map/sweeps/pallas_call | solution.py:411
  86.5 7.7 %correct.1 = f32[1,3,8,16,2048]{4,3,2,1,0:T(8,128)} custom-call(f32[3,16,8,2048]{3,2,1,0:T(8,128)S(1)} %get-tuple-element.7.vv_hbm, f32[3,10,8,512]{3,2,1,0:T(8,128)S(1)} %get-tuple-element.8.d_ref), custom_call_target="tpu_custom_call" | custom-call | tf_op jit(solution)/shard_map/correct/pallas_call | solution.py:430
where the time goes:
time: 94.4 us; the launch traced here: 94.2 us
  Pallas kernels  94.2 us (100%)
    pallas_call x1, Pallas kernels, on_device(): pl.pallas_call(main_kernel, name='sweeps', out_shape=(jax.ShapeDtypeStruc...  86.5 us
    pallas_call x1, Pallas kernels, on_device(): pl.pallas_call(correct_kernel, name='correct', out_shape=jax.ShapeDtypeSt...  7.69 us

commit v1 on v0

--- a/solution.py
+++ b/solution.py
@@ -13,11 +13,29 @@
 F32 = jnp.float32
 
 
-def fine_rate(above, center, below):
+def neighbour_sum(above, center, below):
     lanes = center.shape[-1]
     beside = above + below + pltpu.roll(center, 1, 0) + pltpu.roll(center, 7, 0)
-    beside = beside + pltpu.roll(center, 1, 1) + pltpu.roll(center, lanes - 1, 1)
-    return beside - center * (4.0 + 2.0 * (center * center))
+    return beside + pltpu.roll(center, 1, 1) + pltpu.roll(center, lanes - 1, 1)
+
+
+def cube(value):
+    return value * value * value
+
+
+def combine(weights, terms):
+    total = weights[0] * terms[0]
+    for weight, term in zip(weights[1:], terms[1:]):
+        total = total + weight * term
+    return total
+
+
+def each(count, body, unroll=1):
+    def step(k, carry):
+        body(k)
+        return carry
+
+    lax.fori_loop(0, count, step, 0, unroll=unroll)
 
 
 def iotas():
@@ -58,29 +76,80 @@
     return jnp.concatenate(out, axis=1)
 
 
-def restrict_row(pair_sum, staging):
-    sub, lane = iotas()
-    tiles = split_tiles(pair_sum)
+def packed_halves(row, staging):
+    tiles = split_tiles(row)
     half = len(tiles) // 2
     for t in range(half):
         staging[pl.ds(16 * t, 8), :] = tiles[t]
         staging[pl.ds(16 * t + 8, 8), :] = tiles[t + half]
-    packed = [
-        staging[pl.ds(16 * t, 8, stride=2), :] + staging[pl.ds(16 * t + 1, 8, stride=2), :]
-        for t in range(half)
-    ]
-    index = jnp.where(lane < 64, 2 * lane, 2 * lane - 127)
+    even = [staging[pl.ds(16 * t, 8, stride=2), :] for t in range(half)]
+    odd = [staging[pl.ds(16 * t + 1, 8, stride=2), :] for t in range(half)]
+    return even, odd
+
+
+def decimate_index(lane):
+    return jnp.where(lane < 64, 2 * lane, 2 * lane - 127)
+
+
+def lane_pairs(packed, lane):
     out = []
-    for t in range(half // 2):
+    for t in range(len(packed) // 2):
         p, q = packed[2 * t], packed[2 * t + 1]
         mixed = jnp.where(lane % 2 == 0, p + pltpu.roll(p, 127, 1), q + pltpu.roll(q, 1, 1))
-        out.append(0.125 * take(mixed, index, 1))
-    return jnp.concatenate(out, axis=1)
+        out.append(take(mixed, decimate_index(lane), 1))
+    return out
+
+
+def lane_even_odd(packed, lane):
+    even, odd = [], []
+    for t in range(len(packed) // 2):
+        p, q = packed[2 * t], packed[2 * t + 1]
+        even.append(take(jnp.where(lane % 2 == 0, p, pltpu.roll(q, 1, 1)), decimate_index(lane), 1))
+        odd.append(take(jnp.where(lane % 2 == 0, pltpu.roll(p, 127, 1), q), decimate_index(lane), 1))
+    return even, odd
+
+
+def restrict_row(pair_sum, staging):
+    _, lane = iotas()
+    even, odd = packed_halves(pair_sum, staging)
+    sums = lane_pairs([a + b for a, b in zip(even, odd)], lane)
+    return jnp.concatenate([0.125 * v for v in sums], axis=1)
+
+
+def coarse_terms(fields, staging):
+    sub, lane = iotas()
+    up_index = (sub // 4) * 4 + (sub + 1) % 4
+    down_index = (sub // 4) * 4 + (sub + 3) % 4
+    nodes, inner, evens, odds = [], [], [], []
+    for n, (before, a, b, after) in enumerate(fields):
+        total = a + b
+        rest = (before + after) - total - 2.0 * (cube(a) + cube(b))
+        even, odd = packed_halves(total, staging.at[2 * n])
+        rest_even, rest_odd = packed_halves(rest, staging.at[2 * n + 1])
+        count = len(even)
+        inner.append(
+            [
+                rest_even[t] + rest_odd[t] + take(odd[t], down_index, 0) + take(even[t], up_index, 0)
+                for t in range(count)
+            ]
+        )
+        lane_even, lane_odd = lane_even_odd([even[t] + odd[t] for t in range(count)], lane)
+        evens.append(lane_even)
+        odds.append(lane_odd)
+        nodes.append(jnp.concatenate([0.125 * (p + q) for p, q in zip(lane_even, lane_odd)], axis=1))
+    sums = []
+    for weights in WEIGHTS:
+        weights = [0.125 * STEP * w for w in weights]
+        body = lane_pairs([combine(weights, v) for v in zip(*inner)], lane)
+        left, _ = lane_neighbours([combine(weights, v) for v in zip(*odds)], lane)
+        _, right = lane_neighbours([combine(weights, v) for v in zip(*evens)], lane)
+        sums.append(jnp.concatenate([b + l + r for b, l, r in zip(body, left, right)], axis=1))
+    return nodes, sums
 
 
 def main_kernel(
     u_hbm, vv_hbm, d_hbm,
-    ub, v1, tt, f0, v2, g1, c0, c1, c2, c2p, a0, a1, w0, w1, w2, dd, staging,
+    ub, bb, p0, kk, q1, v1, mm, p2, v2, c0, c1, c2, c2p, a0, a1, w0, w1, w2, dd, staging,
     load_sem, u_send, u_recv, h_send, h_recv, w_send, w_recv, v_send, v_recv, p_send, p_recv, out_sem,
 ):
     tm, sp = lax.axis_index("tm"), lax.axis_index("space")
@@ -100,13 +169,6 @@
     def edge_row(k):
         return jnp.where(k < 3, k, k + 10)
 
-    def each(count, body):
-        def step(k, carry):
-            body(k)
-            return carry
-
-        lax.fori_loop(0, count, step, 0)
-
     def load_edges(k):
         for m in range(3):
             load(m, edge_row(k)).start()
@@ -150,70 +212,61 @@
     u_down.start()
     each(10, wait_inner)
 
+    weights = [STEP * w for w in WEIGHTS[0]]
+    later_weights = [STEP * w for w in WEIGHTS[1]]
+    later_weights[1] = later_weights[1] - half_step
+
+    def local_terms(r):
+        nodes = [ub[m, r + 3] for m in range(3)]
+        cubes = [cube(v) for v in nodes]
+        mixed = combine(weights, nodes)
+        bb[r + 3] = mixed
+        return nodes[0] - 4.0 * mixed + combine([-2.0 * w for w in weights], cubes), nodes, cubes
+
+    def local_terms_near(r):
+        p0[r + 2], nodes, cubes = local_terms(r)
+        kk[r + 2] = combine(later_weights, nodes)
+        q1[r + 2] = combine([-2.0 * w for w in later_weights], cubes)
+
     def first_sweep(r):
-        rates = [fine_rate(ub[m, r + 2], ub[m, r + 3], ub[m, r + 4]) for m in range(3)]
-        (a, b, c), (d, e, f) = WEIGHTS
-        v1[r + 2] = ub[0, r + 3] + (STEP * a) * rates[0] + (STEP * b) * rates[1] + (STEP * c) * rates[2]
-        return rates, (STEP * d) * rates[0] + (STEP * e - half_step) * rates[1] + (STEP * f) * rates[2]
-
-    def first_sweep_inner(r):
-        rates, rest = first_sweep(r)
-        f0[r] = rates[0]
-        tt[r + 1] = rest
+        value = p0[r + 2] + neighbour_sum(bb[r + 2], bb[r + 3], bb[r + 4])
+        mixed = half_step * value + kk[r + 2]
+        v1[r + 2] = value
+        mm[r + 2] = mixed
+        p2[r + 2] = value + q1[r + 2] - 4.0 * mixed - STEP * cube(value)
 
     def second_sweep(r):
-        rate = fine_rate(v1[r + 1], v1[r + 2], v1[r + 3])
-        v2[r + 1] = v1[r + 2] + half_step * rate + tt[r + 1]
-        return rate
-
-    def second_sweep_inner(r):
-        g1[r] = second_sweep(r)
-
-    def restrict_start(i):
-        c0[i + 1] = restrict_row(ub[0, 2 * i + 3] + ub[0, 2 * i + 4], staging.at[0])
-        c1[i + 1] = restrict_row(v1[2 * i + 2] + v1[2 * i + 3], staging.at[1])
-
-    def third_sweep(i):
+        v2[r + 1] = p2[r + 2] + neighbour_sum(mm[r + 1], mm[r + 2], mm[r + 3])
+
+    def restrict_rim(k):
+        i = 9 * k - 1
+        c0[i + 1] = restrict_row(ub[0, 2 * i + 3] + ub[0, 2 * i + 4], staging.at[2 * k])
+        c1[i + 1] = restrict_row(v1[2 * i + 2] + v1[2 * i + 3], staging.at[2 * k + 1])
+
+    def coarse_row(i):
         r = 2 * i
-        (a, b, c), (d, e, f) = WEIGHTS
-        sums = [0.0, 0.0]
-        for k in range(2):
-            g2 = fine_rate(v2[r + k], v2[r + k + 1], v2[r + k + 2])
-            sums[0] = sums[0] + (STEP * a) * f0[r + k] + (STEP * b) * g1[r + k] + (STEP * c) * g2
-            sums[1] = sums[1] + (STEP * d) * f0[r + k] + (STEP * e) * g1[r + k] + (STEP * f) * g2
-        a0[i + 2] = restrict_row(sums[0], staging.at[2])
-        a1[i + 1] = restrict_row(sums[1], staging.at[3])
-        c2[i + 1] = restrict_row(v2[r + 1] + v2[r + 2], staging.at[4])
-
-    each(14, lambda k: first_sweep_inner(k + 1))
-    each(12, lambda k: second_sweep_inner(k + 2))
-
-    def inner_pairs(k):
-        restrict_start(k + 2)
-        third_sweep(k + 2)
-
-    each(4, inner_pairs)
+        fields = [
+            [ub[0, r + k] for k in range(2, 6)],
+            [v1[r + k] for k in range(1, 5)],
+            [v2[r + k] for k in range(4)],
+        ]
+        (c0[i + 1], c1[i + 1], c2[i + 1]), (a0[i + 2], a1[i + 1]) = coarse_terms(fields, staging)
+
+    each(16, local_terms_near, 4)
+    each(14, lambda k: first_sweep(k + 1), 7)
+    each(12, lambda k: second_sweep(k + 2), 6)
+    each(4, lambda k: coarse_row(k + 2), 2)
 
     u_up.wait_recv()
     u_down.wait_recv()
 
-    def first_rim(k):
-        first_sweep_inner(15 * k)
-
-    def first_far(k):
-        r = 17 * k - 1
-        tt[r + 1] = first_sweep(r)[1]
-
-    def first_farthest(k):
-        first_sweep(19 * k - 2)
-
-    each(2, first_rim)
-    each(2, first_far)
-    each(2, first_farthest)
-    each(4, lambda k: second_sweep_inner(jnp.where(k < 2, k, k + 12)))
-    each(2, lambda k: second_sweep(17 * k - 1))
-    each(4, lambda k: third_sweep(jnp.where(k < 2, k, k + 4)))
-    each(6, lambda k: restrict_start(jnp.where(k < 3, k - 1, k + 3)))
+    each(4, lambda k: local_terms_near(jnp.where(k < 2, k - 2, k + 14)), 4)
+    for r in (-3, 18):
+        local_terms(r)
+    each(6, lambda k: first_sweep(jnp.where(k < 3, k - 2, k + 12)), 6)
+    each(6, lambda k: second_sweep(jnp.where(k < 3, k - 1, k + 11)), 6)
+    each(4, lambda k: coarse_row(jnp.where(k < 2, k, k + 4)), 2)
+    each(2, restrict_rim, 2)
 
     def edge_sends(rows, t):
         up = remote(rows.at[pl.ds(5, 3)], w0.at[pl.ds(0, 3)], w_send.at[0], w_recv.at[0], t, right)
@@ -243,7 +296,7 @@
         a0[k + 2] = a0[k + 2] - half_step * coarse_rate(c0[k], c0[k + 1], c0[k + 2])
         a1[k + 1] = a1[k + 1] - half_step * coarse_rate(c1[k], c1[k + 1], c1[k + 2])
 
-    each(8, add_start)
+    each(8, add_start, 8)
     for copy in a_halos + c2_halos:
         copy.start()
 
@@ -286,8 +339,8 @@
     def finish(k):
         w2[k] = w1[k + 1] + half_step * coarse_rate(w1[k], w1[k + 1], w1[k + 2]) + a1[k]
 
-    each(12, middle)
-    each(10, finish)
+    each(12, middle, 12)
+    each(10, finish, 10)
 
     @pl.when(not_last)
     def _():
@@ -373,32 +426,25 @@
                 g75[k, :, columns] = 0.75 * value
                 g25[k, :, columns] = 0.25 * value
 
-    def node(m, carry):
-        def spread_step(k, inner):
-            spread(m, k)
-            return inner
-
-        lax.fori_loop(0, 10, spread_step, 0)
+    def node(m):
+        each(10, lambda k: spread(m, k), 2)
         load(m).wait()
 
-        def rows(k, inner):
+        def rows(k):
             vb[m, 2 * k] = vb[m, 2 * k] + g75[k + 1] + g25[k]
             vb[m, 2 * k + 1] = vb[m, 2 * k + 1] + g75[k + 1] + g25[k + 2]
             store(m, 2 * k).start()
             store(m, 2 * k + 1).start()
-            return inner
-
-        lax.fori_loop(0, 8, rows, 0)
-        return carry
-
-    lax.fori_loop(0, 3, node, 0)
-
-    def drain(k, carry):
+
+        each(8, rows, 4)
+
+    each(3, node)
+
+    def drain(k):
         for m in range(3):
             store(m, k).wait()
-        return carry
-
-    lax.fori_loop(0, 16, drain, 0)
+
+    each(16, drain)
 
 
 def on_device(node_values):
@@ -418,9 +464,9 @@
         in_specs=[anywhere],
         out_specs=(anywhere, anywhere),
         scratch_shapes=[
-            pltpu.VMEM((3, 22, 8, lanes), F32), fine(20), fine(18), fine(16), fine(18), fine(16),
+            pltpu.VMEM((3, 22, 8, lanes), F32), fine(22), fine(20), fine(20), fine(20), fine(20), fine(20), fine(20), fine(18),
             coarse(10), coarse(10), coarse(10), coarse(10), coarse(12), coarse(10), coarse(14), coarse(12), coarse(10),
-            pltpu.VMEM((3, 10, 8, half), F32), pltpu.VMEM((5, lanes // 16, 128), F32),
+            pltpu.VMEM((3, 10, 8, half), F32), pltpu.VMEM((6, lanes // 16, 128), F32),
             dma(3, 16), dma(2), dma(2), dma(6), dma(6), dma(3), dma(3), dma(1), dma(1), dma(1), dma(1), dma(4),
         ],
         compiler_params=pltpu.CompilerParams(

time: 94.4 us -> 82.6 us (0.87)
  the two profiles are of different devices: /device:TPU:31 before, /device:TPU:6 now
where the time goes in v1:
time: 82.6 us; the launch traced here: 82.2 us
  Pallas kernels  82.1 us (99%)
    pallas_call x1, Pallas kernels, on_device(): pl.pallas_call(main_kernel, name='sweeps', out_shape=(jax.ShapeDtypeStruc...  76.8 us
    pallas_call x1, Pallas kernels, on_device(): pl.pallas_call(correct_kernel, name='correct', out_shape=jax.ShapeDtypeSt...  5.35 us

profile of v1, /device:TPU:6, one launch (start us, length us, event | category | flops | bytes accessed | tf_op | source)
XLA Modules:
  0.0 82.2 jit_solution(1558688736147372580)
XLA Ops:
  0.0 76.8 %sweeps.1 = (f32[3,16,8,2048]{3,2,1,0:T(8,128)S(1)}, f32[3,10,8,512]{3,2,1,0:T(8,128)S(1)}) custom-call(f32[1,3,8,16,2048]{4,3,2,1,0:T(8,128)} %u_hbm.1), custom_call_target="tpu_custom_call" | custom-call | tf_op jit(solution)/shard_map/sweeps/pallas_call | solution.py:457
  76.8 5.4 %correct.1 = f32[1,3,8,16,2048]{4,3,2,1,0:T(8,128)} custom-call(f32[3,16,8,2048]{3,2,1,0:T(8,128)S(1)} %get-tuple-element.7.vv_hbm, f32[3,10,8,512]{3,2,1,0:T(8,128)S(1)} %get-tuple-element.8.d_ref), custom_call_target="tpu_custom_call" | custom-call | tf_op jit(solution)/shard_map/correct/pallas_call | solution.py:476

commit v2 on v1

--- a/solution.py
+++ b/solution.py
@@ -10,6 +10,10 @@
 STEP = 0.25
 WEIGHTS = ((5.0 / 24.0, 1.0 / 3.0, -1.0 / 24.0), (-1.0 / 24.0, 1.0 / 3.0, 5.0 / 24.0))
 MESH = pl.DeviceIdType.MESH
+GROUP = 4
+EARLY = 2
+BLOCKS = ((2, 3, 4, 5), (0, 1, 6, 7))
+PLACE = {r: (b, k) for b, rows in enumerate(BLOCKS) for k, r in enumerate(rows)}
 F32 = jnp.float32
 
 
@@ -74,6 +78,41 @@
         beside = a[i] + b[i] + take(c[i], up_index, 0) + take(c[i], down_index, 0) + left[i] + right[i]
         out.append(0.25 * beside + c[i] * (0.5 - 2.0 * (c[i] * c[i])))
     return jnp.concatenate(out, axis=1)
+
+
+def ring_rate(above, center, below):
+    sub, _ = iotas()
+    up_index = (sub // 4) * 4 + (sub + 1) % 4
+    down_index = (sub // 4) * 4 + (sub + 3) % 4
+    beside = above + below + pltpu.roll(center, 1, 1) + pltpu.roll(center, 255, 1)
+    depth = [take(t, up_index, 0) + take(t, down_index, 0) for t in split_tiles(center)]
+    beside = beside + jnp.concatenate(depth, axis=1)
+    return 0.25 * beside + center * (0.5 - 2.0 * (center * center))
+
+
+def strip_of(tiles, t, lane):
+    after = tiles[t + 1] if t + 1 < len(tiles) else pltpu.roll(tiles[0], 4, 0)
+    before = tiles[t - 1] if t > 0 else pltpu.roll(tiles[-1], 4, 0)
+    return jnp.where(lane < 64, after, before)
+
+
+def join_strips(strips, lane):
+    block = ((lane + 16) // 32) % 4
+    joined = strips[0]
+    for k in range(1, 4):
+        joined = jnp.where(block == k, pltpu.roll(strips[k], 32 * k, 1), joined)
+    return joined
+
+
+def put_block(ref, rows, strips, lane):
+    ref[0] = join_strips(strips, lane)
+    for k in range(4):
+        ref[k + 1] = rows[k]
+
+
+def get_row(ref, k):
+    strip = pltpu.roll(ref[0], (128 - 32 * k) % 128, 1)
+    return jnp.concatenate([ref[k + 1], strip], axis=1)
 
 
 def packed_halves(row, staging):
@@ -149,14 +188,19 @@
 
 def main_kernel(
     u_hbm, vv_hbm, d_hbm,
-    ub, bb, p0, kk, q1, v1, mm, p2, v2, c0, c1, c2, c2p, a0, a1, w0, w1, w2, dd, staging,
-    load_sem, u_send, u_recv, h_send, h_recv, w_send, w_recv, v_send, v_recv, p_send, p_recv, out_sem,
+    ub, bb, p0, kk, q1, v1, mm, p2, v2, vin, c0, c1, c2, c2p, a0, a1, pack, cpack, wpack, rx, wx, w0, w1, res, home, dd, staging,
+    load_sem, u_send, u_recv, h_send, h_recv, a_send, a_recv, c_send, w_send, w_recv, r_send, r_recv, v_send, v_recv,
+    p_send, p_recv, out_sem,
 ):
     tm, sp = lax.axis_index("tm"), lax.axis_index("space")
     n_tm, n_sp = lax.axis_size("tm"), lax.axis_size("space")
     left, right = lax.rem(sp + n_sp - 1, n_sp), lax.rem(sp + 1, n_sp)
     not_first, not_last = tm > 0, tm < n_tm - 1
     half_step = 0.5 * STEP
+    team = GROUP * (tm // GROUP)
+    spot = tm - team
+    first_team = tm < GROUP
+    sides = ((left, 2), (sp, 1), (right, 0))
 
     def load(m, r):
         return pltpu.make_async_copy(u_hbm.at[0, m, :, r, :], ub.at[m, r + 3], load_sem.at[m, r])
@@ -181,21 +225,32 @@
     each(10, load_inner)
 
     barrier = pltpu.get_barrier_semaphore()
-    for s in (left, right):
-        pl.semaphore_signal(barrier, inc=1, device_id=(tm, s), device_id_type=MESH)
-
-    @pl.when(not_first)
-    def _():
-        for s in (left, sp, right):
-            pl.semaphore_signal(barrier, inc=1, device_id=(tm - 1, s), device_id_type=MESH)
-
-    @pl.when(not_last)
-    def _():
-        pl.semaphore_wait(barrier, 5)
-
-    @pl.when(jnp.logical_not(not_last))
-    def _():
-        pl.semaphore_wait(barrier, 2)
+    for d in range(GROUP):
+        mate = team + lax.rem(spot + d, GROUP)
+        for s, _ in sides:
+            if d > 0 or s is not sp:
+                pl.semaphore_signal(barrier, inc=1, device_id=(mate, s), device_id_type=MESH)
+
+    @pl.when(jnp.logical_not(first_team))
+    def _():
+        for s, _ in sides:
+            pl.semaphore_signal(barrier, inc=1, device_id=(tm - GROUP, s), device_id_type=MESH)
+
+    @pl.when(tm == GROUP)
+    def _():
+        pl.semaphore_signal(barrier, inc=1, device_id=(tm - 1, sp), device_id_type=MESH)
+
+    @pl.when(tm < GROUP - 1)
+    def _():
+        pl.semaphore_wait(barrier, 3 * GROUP + 2)
+
+    @pl.when(tm == GROUP - 1)
+    def _():
+        pl.semaphore_wait(barrier, 3 * GROUP + 3)
+
+    @pl.when(jnp.logical_not(first_team))
+    def _():
+        pl.semaphore_wait(barrier, 3 * GROUP - 1)
 
     def wait_edges(k):
         for m in range(3):
@@ -252,10 +307,112 @@
         ]
         (c0[i + 1], c1[i + 1], c2[i + 1]), (a0[i + 2], a1[i + 1]) = coarse_terms(fields, staging)
 
+    _, lane = iotas()
+    is_first = jnp.logical_not(not_first)
+
+    def pack_rows(rows, place):
+        tiles = [split_tiles(row) for row in rows]
+        for t in range(GROUP):
+            put_block(place(t), [v[t] for v in tiles], [strip_of(v, t, lane) for v in tiles], lane)
+
+    def start_copies(piece, go):
+        for d in range(GROUP):
+            keeper = lax.rem(spot + d, GROUP)
+            for s, p in sides:
+                if p == piece and (d > 0 or p != 1):
+                    copy = remote(
+                        cpack.at[keeper], wx.at[p], c_send.at[d, p], w_recv.at[p], team + keeper, s
+                    )
+                    go(copy)
+
+    def terms_copy(block, fields, keeper, slot, m, piece, s):
+        return remote(
+            pack.at[block, keeper, pl.ds(0, fields)], rx.at[block, m, piece, pl.ds(0, fields)],
+            a_send.at[block, slot, piece], a_recv.at[block, m, piece], team + keeper, s,
+        )
+
+    def sized(block, m, go):
+        if block == 0:
+            pl.when(m < 2)(lambda: go(2))
+            pl.when(m == 2)(lambda: go(1))
+        else:
+            pl.when(m < 3)(lambda: go(2))
+            pl.when(m == 3)(lambda: go(1))
+
+    def terms_copies(block, go):
+        def mate(d):
+            keeper = lax.rem(spot + d, GROUP)
+
+            @pl.when(d > 0)
+            def _():
+                go(terms_copy(block, 2, keeper, d, spot, 1, sp))
+
+            def beside(fields):
+                go(terms_copy(block, fields, keeper, d, spot, 2, left))
+                go(terms_copy(block, fields, keeper, d, spot, 0, right))
+
+            sized(block, spot, beside)
+
+        each(GROUP, mate)
+
+    def wait_terms(block):
+        def slice_terms(m):
+            @pl.when(m != spot)
+            def _():
+                terms_copy(block, 2, spot, 0, m, 1, left).wait_recv()
+
+            def beside(fields):
+                for piece in (0, 2):
+                    terms_copy(block, fields, spot, 0, m, piece, left).wait_recv()
+
+            sized(block, m, beside)
+
+        each(GROUP, slice_terms)
+
+    def send_terms(block):
+        for k in BLOCKS[block]:
+            a0[k + 2] = a0[k + 2] - half_step * coarse_rate(c0[k], c0[k + 1], c0[k + 2])
+            a1[k + 1] = a1[k + 1] - half_step * coarse_rate(c1[k], c1[k + 1], c1[k + 2])
+        pack_rows([a0[k + 2] for k in BLOCKS[block]], lambda t: pack.at[block, t, 0])
+        pack_rows([a1[k + 1] for k in BLOCKS[block]], lambda t: pack.at[block, t, 1])
+        terms_copies(block, lambda copy: copy.start())
+        rx[block, spot, 1] = pack[block, spot]
+
+    def restrict_first(i):
+        c0[i + 1] = restrict_row(ub[0, 2 * i + 3] + ub[0, 2 * i + 4], staging.at[i % 4])
+
+    for k in range(8):
+        restrict_first(k)
+
+    @pl.when(is_first)
+    def _():
+        for block in range(2):
+            pack_rows([c0[k + 1] for k in BLOCKS[block]], lambda t: cpack.at[t, block])
+        for piece in range(3):
+            start_copies(piece, lambda copy: copy.start())
+        wx[1] = cpack[0]
+
     each(16, local_terms_near, 4)
     each(14, lambda k: first_sweep(k + 1), 7)
     each(12, lambda k: second_sweep(k + 2), 6)
+
+    def v_part(index, start, count):
+        return remote(
+            v2.at[pl.ds(start + 1, count)], vin.at[pl.ds(start, count)], v_send.at[index], v_recv.at[index], tm + 1, sp
+        )
+
+    v_ranges = ((2, EARLY), (0, 2), (2 + EARLY, 14 - EARLY))
+    v_parts = [v_part(n, *rows) for n, rows in enumerate(v_ranges)]
+
+    @pl.when(not_last)
+    def _():
+        v_parts[0].start()
+
+
     each(4, lambda k: coarse_row(k + 2), 2)
+    for n, i in enumerate((1, 6)):
+        c1[i + 1] = restrict_row(v1[2 * i + 2] + v1[2 * i + 3], staging.at[n])
+    send_terms(0)
 
     u_up.wait_recv()
     u_down.wait_recv()
@@ -268,131 +425,183 @@
     each(4, lambda k: coarse_row(jnp.where(k < 2, k, k + 4)), 2)
     each(2, restrict_rim, 2)
 
-    def edge_sends(rows, t):
-        up = remote(rows.at[pl.ds(5, 3)], w0.at[pl.ds(0, 3)], w_send.at[0], w_recv.at[0], t, right)
-        down = remote(rows.at[pl.ds(0, 3)], w0.at[pl.ds(11, 3)], w_send.at[1], w_recv.at[1], t, left)
-        return up, down
-
-    own_c0, own_w2 = c0.at[pl.ds(1, 8)], w2.at[pl.ds(1, 8)]
-    start_up, start_down = edge_sends(own_c0, tm)
-    next_up, next_down = edge_sends(own_w2, tm + 1)
-    next_own = remote(own_w2, w0.at[pl.ds(3, 8)], w_send.at[2], w_recv.at[2], tm + 1, sp)
-    is_first = jnp.logical_not(not_first)
-
-    @pl.when(is_first)
-    def _():
-        start_up.start()
-        start_down.start()
-
-    def halo_sends(index, field, rows, own):
-        up = remote(field.at[pl.ds(own + 8 - rows, rows)], field.at[pl.ds(own - rows, rows)], h_send.at[index], h_recv.at[index], tm, right)
-        down = remote(field.at[pl.ds(own, rows)], field.at[pl.ds(own + 8, rows)], h_send.at[index + 1], h_recv.at[index + 1], tm, left)
-        return [up, down]
-
-    c2_halos = halo_sends(0, c2, 1, 1)
-    a_halos = halo_sends(2, a0, 2, 2) + halo_sends(4, a1, 1, 1)
-
-    def add_start(k):
-        a0[k + 2] = a0[k + 2] - half_step * coarse_rate(c0[k], c0[k + 1], c0[k + 2])
-        a1[k + 1] = a1[k + 1] - half_step * coarse_rate(c1[k], c1[k + 1], c1[k + 2])
-
-    each(8, add_start, 8)
-    for copy in a_halos + c2_halos:
-        copy.start()
-
+    send_terms(1)
+
+    @pl.when(not_last)
+    def _():
+        for copy in v_parts[1:]:
+            copy.start()
+
+
+    c2_up = remote(c2.at[pl.ds(8, 1)], c2.at[pl.ds(0, 1)], h_send.at[0], h_recv.at[0], tm, right)
+    c2_down = remote(c2.at[pl.ds(1, 1)], c2.at[pl.ds(9, 1)], h_send.at[1], h_recv.at[1], tm, left)
+    c2_up.start()
+    c2_down.start()
     v1_out = pltpu.make_async_copy(v1.at[pl.ds(2, 16)], vv_hbm.at[1], out_sem.at[0])
     v2_out = pltpu.make_async_copy(v2.at[pl.ds(1, 16)], vv_hbm.at[2], out_sem.at[1])
     u0_out = pltpu.make_async_copy(ub.at[0, pl.ds(3, 16)], vv_hbm.at[0], out_sem.at[2])
-    v_next = remote(v2.at[pl.ds(1, 16)], vv_hbm.at[0], v_send.at[0], v_recv.at[0], tm + 1, sp)
+    p_next = [
+        remote(c2.at[pl.ds(k, 1)], c2p.at[pl.ds(k, 1)], p_send.at[n], p_recv.at[n], tm + 1, sp) for n, k in enumerate((0, 9))
+    ]
     v1_out.start()
     v2_out.start()
 
-    early = tm >= n_tm // 2
-
     @pl.when(is_first)
     def _():
         u0_out.start()
-        w0[pl.ds(3, 8)] = c0[pl.ds(1, 8)]
-
-    @pl.when(not_last & early)
-    def _():
-        v_next.start()
-
-    for copy in a_halos + c2_halos:
-        copy.wait_recv()
-    p_next = remote(c2, c2p, p_send.at[0], p_recv.at[0], tm + 1, sp)
+
+    wait_terms(0)
+    wait_terms(1)
+    c2_up.wait_recv()
+    c2_down.wait_recv()
 
     @pl.when(not_last)
     def _():
-        p_next.start()
+        for copy in p_next:
+            copy.start()
+
+    for piece in (0, 2):
+        remote(wpack, wx.at[piece], w_send.at[piece], w_recv.at[piece], tm, left).wait_recv()
 
     @pl.when(not_first)
     def _():
-        next_own.wait_recv()
-
-    start_up.wait_recv()
-    start_down.wait_recv()
-
-    def middle(k):
-        w1[k] = w0[k + 1] + half_step * coarse_rate(w0[k], w0[k + 1], w0[k + 2]) + a0[k]
-
-    def finish(k):
-        w2[k] = w1[k + 1] + half_step * coarse_rate(w1[k], w1[k + 1], w1[k + 2]) + a1[k]
-
-    each(12, middle, 12)
-    each(10, finish, 10)
+        remote(wpack, wx.at[1], w_send.at[1], w_recv.at[1], tm, left).wait_recv()
+
+    for piece in range(3):
+        for r in range(8):
+            block, k = PLACE[r]
+            w0[8 * piece + r] = get_row(wx.at[piece, block], k)
+
+    def go_home(m, go, here):
+        owner = team + m
+        own = remote(res.at[m], home.at[:, pl.ds(1, 8), spot], r_send.at[m, 1], r_recv.at[spot, 1], owner, sp)
+        up = remote(res.at[m, :, 7], home.at[:, 0, spot], r_send.at[m, 0], r_recv.at[spot, 0], owner, right)
+        down = remote(res.at[m, :, 0], home.at[:, 9, spot], r_send.at[m, 2], r_recv.at[spot, 2], owner, left)
+        go(up)
+        go(down)
+
+        @pl.when(m != spot)
+        def _():
+            go(own)
+
+        @pl.when(m == spot)
+        def _():
+            here()
+
+    def sweep(m):
+        def term(field, k):
+            block, place = PLACE[k % 8]
+            return get_row(rx.at[block, m, k // 8, field], place)
+
+        def keep(field, k, value):
+            if 8 <= k < 16:
+                res[m, field, k - 8] = value[:, :128]
+
+        for k in range(8, 16):
+            keep(0, k, w0[k])
+        for k in range(1, 23):
+            value = w0[k] + half_step * ring_rate(w0[k - 1], w0[k], w0[k + 1]) + term(0, k)
+            w1[k] = value
+            keep(1, k, value)
+        for k in range(2, 22):
+            value = w1[k] + half_step * ring_rate(w1[k - 1], w1[k], w1[k + 1]) + term(1, k)
+            w0[k] = value
+            keep(2, k, value)
+
+        def here():
+            home[:, pl.ds(1, 8), spot] = res[m]
+
+        go_home(m, lambda copy: copy.start(), here)
+
+    each(GROUP, sweep)
+
+    group_sends = [
+        remote(wpack, wx.at[piece], w_send.at[piece], w_recv.at[piece], tm + GROUP, s) for s, piece in sides
+    ]
+
+    @pl.when(first_team)
+    def _():
+        rows = [split_tiles(w0[k]) for k in range(8, 16)]
+        for block in range(2):
+            put_block(wpack.at[block], [rows[r][0] for r in BLOCKS[block]], [rows[r][1] for r in BLOCKS[block]], lane)
+        for copy in group_sends:
+            copy.start()
+
+    def wait_home(t):
+        for piece, source, target in (
+            (0, res.at[0, :, 7], home.at[:, 0, t]),
+            (2, res.at[0, :, 0], home.at[:, 9, t]),
+        ):
+            remote(source, target, r_send.at[0, piece], r_recv.at[t, piece], tm, left).wait_recv()
+
+        @pl.when(t != spot)
+        def _():
+            remote(res.at[0], home.at[:, pl.ds(1, 8), t], r_send.at[0, 1], r_recv.at[t, 1], tm, left).wait_recv()
+
+    each(GROUP, wait_home)
+
+    for t in range(GROUP):
+        columns = pl.ds(128 * t, 128)
+        dd[1, :, :, columns] = home[1, :, t] - c1[:, :, columns]
+        dd[2, :, :, columns] = home[2, :, t] - c2[:, :, columns]
+
+    d_out = [
+        pltpu.make_async_copy(dd.at[pl.ds(1, 2)], d_hbm.at[pl.ds(1, 2)], out_sem.at[3]),
+        pltpu.make_async_copy(dd.at[pl.ds(0, 1)], d_hbm.at[pl.ds(0, 1)], out_sem.at[4]),
+    ]
+    d_out[0].start()
+
+    @pl.when(is_first)
+    def _():
+        dd[0] = jnp.zeros(dd.shape[1:], F32)
+
+    @pl.when(not_first)
+    def _():
+        for copy in v_parts:
+            copy.wait_recv()
+        pltpu.make_async_copy(vin, vv_hbm.at[0], out_sem.at[2]).start()
+        for i in range(8):
+            c2p[i + 1] = restrict_row(vin[2 * i] + vin[2 * i + 1], staging.at[i % 4])
+        for copy in p_next:
+            copy.wait_recv()
+        for t in range(GROUP):
+            columns = pl.ds(128 * t, 128)
+            dd[0, :, :, columns] = home[0, :, t] - c2p[:, :, columns]
+
+    d_out[1].start()
+
+    for copy in (u_up, u_down, c2_up, c2_down):
+        copy.wait_send()
+    for block in range(2):
+        terms_copies(block, lambda copy: copy.wait_send())
+    each(GROUP, lambda m: go_home(m, lambda copy: copy.wait_send(), lambda: None))
+
+    @pl.when(is_first)
+    def _():
+        for piece in range(3):
+            start_copies(piece, lambda copy: copy.wait_send())
+        u0_out.wait()
+
+    @pl.when(first_team)
+    def _():
+        for copy in group_sends:
+            copy.wait_send()
 
     @pl.when(not_last)
     def _():
-        next_own.start()
-        next_up.start()
-        next_down.start()
-
-    @pl.when(not_last & jnp.logical_not(early))
-    def _():
-        v_next.start()
-
-    dd[1] = w1[pl.ds(1, 10)] - c1[...]
-    dd[2] = w2[...] - c2[...]
+        for copy in p_next:
+            copy.wait_send()
+        for copy in v_parts:
+            copy.wait_send()
 
     @pl.when(not_first)
     def _():
-        p_next.wait_recv()
-        dd[0] = w0[pl.ds(2, 10)] - c2p[...]
-
-    @pl.when(is_first)
-    def _():
-        dd[0] = jnp.zeros(dd.shape[1:], F32)
-
-    d_out = pltpu.make_async_copy(dd, d_hbm, out_sem.at[3])
-    d_out.start()
-
-    u_up.wait_send()
-    u_down.wait_send()
-    for copy in a_halos + c2_halos:
-        copy.wait_send()
-
-    @pl.when(is_first)
-    def _():
-        start_up.wait_send()
-        start_down.wait_send()
-        u0_out.wait()
-
-    @pl.when(not_last)
-    def _():
-        next_own.wait_send()
-        next_up.wait_send()
-        next_down.wait_send()
-        p_next.wait_send()
-        v_next.wait_send()
-
-    @pl.when(not_first)
-    def _():
-        v_next.wait_recv()
+        pltpu.make_async_copy(vin, vv_hbm.at[0], out_sem.at[2]).wait()
 
     v1_out.wait()
     v2_out.wait()
-    d_out.wait()
+    for copy in d_out:
+        copy.wait()
 
 
 def correct_kernel(vv_hbm, d_ref, o_hbm, vb, g75, g25, in_sem, out_sem):
@@ -452,6 +661,7 @@
     half = lanes // 4
     fine = lambda n: pltpu.VMEM((n, 8, lanes), F32)
     coarse = lambda n: pltpu.VMEM((n, 8, half), F32)
+    tiles = lambda *n: pltpu.VMEM(n + (8, 128), F32)
     dma = lambda *n: pltpu.SemaphoreType.DMA(n)
     anywhere = pl.BlockSpec(memory_space=pl.ANY)
     vv, dd = pl.pallas_call(
@@ -464,10 +674,13 @@
         in_specs=[anywhere],
         out_specs=(anywhere, anywhere),
         scratch_shapes=[
-            pltpu.VMEM((3, 22, 8, lanes), F32), fine(22), fine(20), fine(20), fine(20), fine(20), fine(20), fine(20), fine(18),
-            coarse(10), coarse(10), coarse(10), coarse(10), coarse(12), coarse(10), coarse(14), coarse(12), coarse(10),
+            pltpu.VMEM((3, 22, 8, lanes), F32), fine(22), fine(20), fine(20), fine(20), fine(20), fine(20), fine(20), fine(18), fine(16),
+            coarse(10), coarse(10), coarse(10), coarse(10), coarse(12), coarse(10),
+            tiles(2, GROUP, 2, 5), tiles(GROUP, 2, 5), tiles(2, 5), tiles(2, GROUP, 3, 2, 5), tiles(3, 2, 5),
+            pltpu.VMEM((24, 8, 256), F32), pltpu.VMEM((24, 8, 256), F32), tiles(GROUP, 3, 8), tiles(3, 10, GROUP),
             pltpu.VMEM((3, 10, 8, half), F32), pltpu.VMEM((6, lanes // 16, 128), F32),
-            dma(3, 16), dma(2), dma(2), dma(6), dma(6), dma(3), dma(3), dma(1), dma(1), dma(1), dma(1), dma(4),
+            dma(3, 16), dma(2), dma(2), dma(2), dma(2), dma(2, GROUP, 3), dma(2, GROUP, 3), dma(GROUP, 3), dma(3), dma(3),
+            dma(GROUP, 3), dma(GROUP, 3), dma(3), dma(3), dma(2), dma(2), dma(5),
         ],
         compiler_params=pltpu.CompilerParams(
             collective_id=0, has_side_effects=True, vmem_limit_bytes=48 * 1024 * 1024

time: 82.6 us -> 61 us (0.74)
  Pallas kernels: 82.1 us -> 60.1 us
    pallas_call x1, Pallas kernels: 76.8 us -> 54.7 us  [on_device(): pl.pallas_call(main_kernel, name='sweeps', out_shape=(jax.ShapeDtypeStruc...]
where the time goes in v2:
time: 61 us; the launch traced here: 60.1 us
  Pallas kernels  60.1 us (99%)
    pallas_call x1, Pallas kernels, on_device(): pl.pallas_call(main_kernel, name='sweeps', out_shape=(jax.ShapeDtypeStruc...  54.7 us
    pallas_call x1, Pallas kernels, on_device(): pl.pallas_call(correct_kernel, name='correct', out_shape=jax.ShapeDtypeSt...  5.35 us

profile of v2, /device:TPU:6, one launch (start us, length us, event | category | flops | bytes accessed | tf_op | source)
XLA Modules:
  0.0 60.1 jit_solution(8277985590120487553)
XLA Ops:
  0.0 54.7 %sweeps.1 = (f32[3,16,8,2048]{3,2,1,0:T(8,128)S(1)}, f32[3,10,8,512]{3,2,1,0:T(8,128)S(1)}) custom-call(f32[1,3,8,16,2048]{4,3,2,1,0:T(8,128)} %u_hbm.1), custom_call_target="tpu_custom_call" | custom-call | tf_op jit(solution)/shard_map/sweeps/pallas_call | solution.py:667
  54.7 5.4 %correct.1 = f32[1,3,8,16,2048]{4,3,2,1,0:T(8,128)} custom-call(f32[3,16,8,2048]{3,2,1,0:T(8,128)S(1)} %get-tuple-element.7.vv_hbm, f32[3,10,8,512]{3,2,1,0:T(8,128)S(1)} %get-tuple-element.8.d_ref), custom_call_target="tpu_custom_call" | custom-call | tf_op jit(solution)/shard_map/correct/pallas_call | solution.py:689

commit v3 on v2

--- a/solution.py
+++ b/solution.py
@@ -11,7 +11,7 @@
 WEIGHTS = ((5.0 / 24.0, 1.0 / 3.0, -1.0 / 24.0), (-1.0 / 24.0, 1.0 / 3.0, 5.0 / 24.0))
 MESH = pl.DeviceIdType.MESH
 GROUP = 4
-EARLY = 2
+ROWS = ((2, 2), (4, 4), (8, 4), (12, 4), (0, 2))
 BLOCKS = ((2, 3, 4, 5), (0, 1, 6, 7))
 PLACE = {r: (b, k) for b, rows in enumerate(BLOCKS) for k, r in enumerate(rows)}
 F32 = jnp.float32
@@ -188,8 +188,8 @@
 
 def main_kernel(
     u_hbm, vv_hbm, d_hbm,
-    ub, bb, p0, kk, q1, v1, mm, p2, v2, vin, c0, c1, c2, c2p, a0, a1, pack, cpack, wpack, rx, wx, w0, w1, res, home, dd, staging,
-    load_sem, u_send, u_recv, h_send, h_recv, a_send, a_recv, c_send, w_send, w_recv, r_send, r_recv, v_send, v_recv,
+    ub, bb, p0, kk, q1, v1, mm, p2, v2, vin, around, relay, c0, c1, c2, c2p, a0, a1, pack, cpack, wpack, rx, wx, w0, w1, res, home, edges, dd, staging,
+    load_sem, u_send, u_recv, e_send, e_recv, h_send, h_recv, a_send, a_recv, c_send, w_send, w_recv, r_send, r_recv, g_send, g_recv, v_send, v_recv, o_send, o_recv, q_send, q_recv,
     p_send, p_recv, out_sem,
 ):
     tm, sp = lax.axis_index("tm"), lax.axis_index("space")
@@ -261,11 +261,12 @@
             load(m, k + 3).wait()
 
     each(6, wait_edges)
-    u_up = remote(ub.at[:, pl.ds(16, 3)], ub.at[:, pl.ds(0, 3)], u_send.at[0], u_recv.at[0], tm, right)
-    u_down = remote(ub.at[:, pl.ds(3, 3)], ub.at[:, pl.ds(19, 3)], u_send.at[1], u_recv.at[1], tm, left)
-    u_up.start()
-    u_down.start()
-    each(10, wait_inner)
+    u_copies = [
+        remote(ub.at[:, pl.ds(18, 1)], ub.at[:, pl.ds(2, 1)], u_send.at[0], u_recv.at[0], tm, right),
+        remote(ub.at[:, pl.ds(3, 1)], ub.at[:, pl.ds(19, 1)], u_send.at[1], u_recv.at[1], tm, left),
+    ]
+    for copy in u_copies:
+        copy.start()
 
     weights = [STEP * w for w in WEIGHTS[0]]
     later_weights = [STEP * w for w in WEIGHTS[1]]
@@ -276,10 +277,7 @@
         cubes = [cube(v) for v in nodes]
         mixed = combine(weights, nodes)
         bb[r + 3] = mixed
-        return nodes[0] - 4.0 * mixed + combine([-2.0 * w for w in weights], cubes), nodes, cubes
-
-    def local_terms_near(r):
-        p0[r + 2], nodes, cubes = local_terms(r)
+        p0[r + 2] = nodes[0] - 4.0 * mixed + combine([-2.0 * w for w in weights], cubes)
         kk[r + 2] = combine(later_weights, nodes)
         q1[r + 2] = combine([-2.0 * w for w in later_weights], cubes)
 
@@ -295,8 +293,7 @@
 
     def restrict_rim(k):
         i = 9 * k - 1
-        c0[i + 1] = restrict_row(ub[0, 2 * i + 3] + ub[0, 2 * i + 4], staging.at[2 * k])
-        c1[i + 1] = restrict_row(v1[2 * i + 2] + v1[2 * i + 3], staging.at[2 * k + 1])
+        c1[i + 1] = restrict_row(v1[2 * i + 2] + v1[2 * i + 3], staging.at[k])
 
     def coarse_row(i):
         r = 2 * i
@@ -305,7 +302,7 @@
             [v1[r + k] for k in range(1, 5)],
             [v2[r + k] for k in range(4)],
         ]
-        (c0[i + 1], c1[i + 1], c2[i + 1]), (a0[i + 2], a1[i + 1]) = coarse_terms(fields, staging)
+        (_, c1[i + 1], c2[i + 1]), (a0[i + 2], a1[i + 1]) = coarse_terms(fields, staging)
 
     _, lane = iotas()
     is_first = jnp.logical_not(not_first)
@@ -381,7 +378,22 @@
     def restrict_first(i):
         c0[i + 1] = restrict_row(ub[0, 2 * i + 3] + ub[0, 2 * i + 4], staging.at[i % 4])
 
-    for k in range(8):
+    each(6, lambda k: local_terms(edge_row(k)), 3)
+    for k in (0, 7):
+        restrict_first(k)
+    for r in (1, 14):
+        first_sweep(r)
+    rim_copies, rows_of = [], (16, 16, 16, 8)
+    for n, (field, offset, up, down) in enumerate(((bb, 3, 14, 1), (v1, 2, 14, 1), (mm, 2, 14, 1), (c0, 1, 7, 0))):
+        up_target, down_target = up + offset - rows_of[n], down + offset + rows_of[n]
+        rim_copies += [
+            remote(field.at[pl.ds(up + offset, 1)], field.at[pl.ds(up_target, 1)], e_send.at[0, n], e_recv.at[0, n], tm, right),
+            remote(field.at[pl.ds(down + offset, 1)], field.at[pl.ds(down_target, 1)], e_send.at[1, n], e_recv.at[1, n], tm, left),
+        ]
+    for copy in rim_copies:
+        copy.start()
+    each(10, wait_inner)
+    for k in range(1, 7):
         restrict_first(k)
 
     @pl.when(is_first)
@@ -392,8 +404,8 @@
             start_copies(piece, lambda copy: copy.start())
         wx[1] = cpack[0]
 
-    each(16, local_terms_near, 4)
-    each(14, lambda k: first_sweep(k + 1), 7)
+    each(10, lambda k: local_terms(k + 3), 5)
+    each(12, lambda k: first_sweep(k + 2), 6)
     each(12, lambda k: second_sweep(k + 2), 6)
 
     def v_part(index, start, count):
@@ -401,36 +413,76 @@
             v2.at[pl.ds(start + 1, count)], vin.at[pl.ds(start, count)], v_send.at[index], v_recv.at[index], tm + 1, sp
         )
 
-    v_ranges = ((2, EARLY), (0, 2), (2 + EARLY, 14 - EARLY))
-    v_parts = [v_part(n, *rows) for n, rows in enumerate(v_ranges)]
+    v_parts = [v_part(n, *rows) for n, rows in enumerate(ROWS)]
+    behind = team + lax.rem(spot + GROUP - 1, GROUP)
+    start, count = ROWS[1]
+    hops = [
+        remote(v2.at[pl.ds(start + 1, count)], around.at[0], o_send.at[0], o_recv.at[0], behind, sp),
+        remote(around.at[0], around.at[1], o_send.at[1], o_recv.at[1], behind, sp),
+        remote(around.at[1], vin.at[pl.ds(start, count)], o_send.at[2], v_recv.at[1], behind, sp),
+    ]
+    goes = [spot != GROUP - 1, spot != GROUP - 2, spot != GROUP - 3]
+
+    def start_hop(n):
+        @pl.when(goes[n])
+        def _():
+            if n > 0:
+                hops[n - 1].wait_recv()
+            hops[n].start()
 
     @pl.when(not_last)
     def _():
         v_parts[0].start()
 
+    start_hop(0)
+
+    relay_in, relay_out = [], []
+    for k, n in enumerate((1, 3)):
+        first, count = ROWS[n]
+        held = relay.at[k]
+        relay_in.append(remote(v2.at[pl.ds(first + 1, count)], held, q_send.at[k], q_recv.at[k], team, sp))
+        relay_out.append(remote(held, vin.at[pl.ds(first, count)], q_send.at[2 + k], v_recv.at[n], tm + GROUP, sp))
+
+    def start_relay(k):
+        @pl.when(is_first)
+        def _():
+            relay_in[k].wait_recv()
+            relay_out[k].start()
+
+    @pl.when(tm == GROUP - 1)
+    def _():
+        relay_in[0].start()
 
     each(4, lambda k: coarse_row(k + 2), 2)
     for n, i in enumerate((1, 6)):
         c1[i + 1] = restrict_row(v1[2 * i + 2] + v1[2 * i + 3], staging.at[n])
     send_terms(0)
 
-    u_up.wait_recv()
-    u_down.wait_recv()
-
-    each(4, lambda k: local_terms_near(jnp.where(k < 2, k - 2, k + 14)), 4)
-    for r in (-3, 18):
+    for copy in u_copies:
+        copy.wait_recv()
+    for r in (-1, 16):
         local_terms(r)
-    each(6, lambda k: first_sweep(jnp.where(k < 3, k - 2, k + 12)), 6)
-    each(6, lambda k: second_sweep(jnp.where(k < 3, k - 1, k + 11)), 6)
-    each(4, lambda k: coarse_row(jnp.where(k < 2, k, k + 4)), 2)
+    for r in (0, 15):
+        first_sweep(r)
+    for r in (1, 14):
+        second_sweep(r)
+    for i in (1, 6):
+        coarse_row(i)
+    for copy in rim_copies:
+        copy.wait_recv()
+    for r in (-1, 16):
+        first_sweep(r)
+    for r in (-1, 0, 15, 16):
+        second_sweep(r)
+    for i in (0, 7):
+        coarse_row(i)
     each(2, restrict_rim, 2)
 
     send_terms(1)
 
     @pl.when(not_last)
     def _():
-        for copy in v_parts[1:]:
-            copy.start()
+        v_parts[2].start()
 
 
     c2_up = remote(c2.at[pl.ds(8, 1)], c2.at[pl.ds(0, 1)], h_send.at[0], h_recv.at[0], tm, right)
@@ -450,8 +502,23 @@
     def _():
         u0_out.start()
 
+    start_hop(1)
+    start_relay(0)
     wait_terms(0)
     wait_terms(1)
+
+    def late_parts():
+        for copy in v_parts[3:]:
+            copy.start()
+
+    @pl.when(not_last & (tm != GROUP - 1))
+    def _():
+        late_parts()
+
+    @pl.when(tm == GROUP - 1)
+    def _():
+        relay_in[1].start()
+
     c2_up.wait_recv()
     c2_down.wait_recv()
 
@@ -459,6 +526,10 @@
     def _():
         for copy in p_next:
             copy.start()
+
+    @pl.when(jnp.logical_not(first_team))
+    def _():
+        start_hop(2)
 
     for piece in (0, 2):
         remote(wpack, wx.at[piece], w_send.at[piece], w_recv.at[piece], tm, left).wait_recv()
@@ -472,21 +543,23 @@
             block, k = PLACE[r]
             w0[8 * piece + r] = get_row(wx.at[piece, block], k)
 
+    last_m = GROUP - 1
+
     def go_home(m, go, here):
         owner = team + m
-        own = remote(res.at[m], home.at[:, pl.ds(1, 8), spot], r_send.at[m, 1], r_recv.at[spot, 1], owner, sp)
-        up = remote(res.at[m, :, 7], home.at[:, 0, spot], r_send.at[m, 0], r_recv.at[spot, 0], owner, right)
-        down = remote(res.at[m, :, 0], home.at[:, 9, spot], r_send.at[m, 2], r_recv.at[spot, 2], owner, left)
-        go(up)
-        go(down)
 
         @pl.when(m != spot)
         def _():
-            go(own)
+            go(remote(res.at[m], home.at[spot], r_send.at[m], r_recv.at[spot], owner, sp))
 
         @pl.when(m == spot)
         def _():
             here()
+
+    end_copies = [
+        remote(res.at[last_m, 2, 8], edges.at[0, spot], g_send.at[0], g_recv.at[spot, 0], team + last_m, right),
+        remote(res.at[last_m, 2, 1], edges.at[1, spot], g_send.at[1], g_recv.at[spot, 1], team + last_m, left),
+    ]
 
     def sweep(m):
         def term(field, k):
@@ -494,10 +567,10 @@
             return get_row(rx.at[block, m, k // 8, field], place)
 
         def keep(field, k, value):
-            if 8 <= k < 16:
-                res[m, field, k - 8] = value[:, :128]
-
-        for k in range(8, 16):
+            if 7 <= k < 17:
+                res[m, field, k - 7] = value[:, :128]
+
+        for k in range(7, 17):
             keep(0, k, w0[k])
         for k in range(1, 23):
             value = w0[k] + half_step * ring_rate(w0[k - 1], w0[k], w0[k + 1]) + term(0, k)
@@ -509,11 +582,13 @@
             keep(2, k, value)
 
         def here():
-            home[:, pl.ds(1, 8), spot] = res[m]
+            home[spot] = res[m]
 
         go_home(m, lambda copy: copy.start(), here)
 
     each(GROUP, sweep)
+    for copy in end_copies:
+        copy.start()
 
     group_sends = [
         remote(wpack, wx.at[piece], w_send.at[piece], w_recv.at[piece], tm + GROUP, s) for s, piece in sides
@@ -527,23 +602,56 @@
         for copy in group_sends:
             copy.start()
 
+    @pl.when(tm == GROUP - 1)
+    def _():
+        for copy in group_sends:
+            copy.wait_send()
+        v_parts[4].start()
+
+    @pl.when(first_team)
+    def _():
+        start_hop(2)
+
+
     def wait_home(t):
-        for piece, source, target in (
-            (0, res.at[0, :, 7], home.at[:, 0, t]),
-            (2, res.at[0, :, 0], home.at[:, 9, t]),
-        ):
-            remote(source, target, r_send.at[0, piece], r_recv.at[t, piece], tm, left).wait_recv()
-
         @pl.when(t != spot)
         def _():
-            remote(res.at[0], home.at[:, pl.ds(1, 8), t], r_send.at[0, 1], r_recv.at[t, 1], tm, left).wait_recv()
+            remote(res.at[0], home.at[t], r_send.at[0], r_recv.at[t], tm, left).wait_recv()
+
+    def vin_out(n):
+        rows = pl.ds(*ROWS[n])
+        return pltpu.make_async_copy(vin.at[rows], vv_hbm.at[0, rows], out_sem.at[5 + n])
+
+    def take_parts(which):
+        for n in which:
+            v_parts[n].wait_recv()
+            vin_out(n).start()
+        for n in which:
+            first, count = ROWS[n]
+            for i in range(first // 2, (first + count) // 2):
+                c2p[i + 1] = restrict_row(vin[2 * i] + vin[2 * i + 1], staging.at[i % 6])
+
+    start_relay(1)
+
+    @pl.when(not_first)
+    def _():
+        take_parts((0, 2))
+        take_parts((1, 3, 4))
 
     each(GROUP, wait_home)
 
     for t in range(GROUP):
         columns = pl.ds(128 * t, 128)
-        dd[1, :, :, columns] = home[1, :, t] - c1[:, :, columns]
-        dd[2, :, :, columns] = home[2, :, t] - c2[:, :, columns]
+        dd[1, :, :, columns] = home[t, 1] - c1[:, :, columns]
+        dd[2, :, :, columns] = home[t, 2] - c2[:, :, columns]
+
+    @pl.when(spot == last_m)
+    def _():
+        for t in range(GROUP):
+            columns = pl.ds(128 * t, 128)
+            for side in range(2):
+                remote(res.at[0, 2, 8], edges.at[side, t], g_send.at[side], g_recv.at[t, side], tm, left).wait_recv()
+                dd[2, 9 * side, :, columns] = edges[side, t] - c2[9 * side, :, columns]
 
     d_out = [
         pltpu.make_async_copy(dd.at[pl.ds(1, 2)], d_hbm.at[pl.ds(1, 2)], out_sem.at[3]),
@@ -557,24 +665,21 @@
 
     @pl.when(not_first)
     def _():
-        for copy in v_parts:
-            copy.wait_recv()
-        pltpu.make_async_copy(vin, vv_hbm.at[0], out_sem.at[2]).start()
-        for i in range(8):
-            c2p[i + 1] = restrict_row(vin[2 * i] + vin[2 * i + 1], staging.at[i % 4])
         for copy in p_next:
             copy.wait_recv()
         for t in range(GROUP):
             columns = pl.ds(128 * t, 128)
-            dd[0, :, :, columns] = home[0, :, t] - c2p[:, :, columns]
+            dd[0, :, :, columns] = home[t, 0] - c2p[:, :, columns]
 
     d_out[1].start()
 
-    for copy in (u_up, u_down, c2_up, c2_down):
+    for copy in (*u_copies, *rim_copies, c2_up, c2_down):
         copy.wait_send()
     for block in range(2):
         terms_copies(block, lambda copy: copy.wait_send())
     each(GROUP, lambda m: go_home(m, lambda copy: copy.wait_send(), lambda: None))
+    for copy in end_copies:
+        copy.wait_send()
 
     @pl.when(is_first)
     def _():
@@ -582,7 +687,7 @@
             start_copies(piece, lambda copy: copy.wait_send())
         u0_out.wait()
 
-    @pl.when(first_team)
+    @pl.when(tm < GROUP - 1)
     def _():
         for copy in group_sends:
             copy.wait_send()
@@ -591,12 +696,33 @@
     def _():
         for copy in p_next:
             copy.wait_send()
-        for copy in v_parts:
+        for n in (0, 2, 4):
+            v_parts[n].wait_send()
+
+    @pl.when(not_last & (tm != GROUP - 1))
+    def _():
+        v_parts[3].wait_send()
+
+    @pl.when(tm == GROUP - 1)
+    def _():
+        for copy in relay_in:
             copy.wait_send()
 
+    @pl.when(is_first)
+    def _():
+        for copy in relay_out:
+            copy.wait_send()
+
+    for n in range(3):
+
+        @pl.when(goes[n])
+        def _():
+            hops[n].wait_send()
+
     @pl.when(not_first)
     def _():
-        pltpu.make_async_copy(vin, vv_hbm.at[0], out_sem.at[2]).wait()
+        for n in range(5):
+            vin_out(n).wait()
 
     v1_out.wait()
     v2_out.wait()
@@ -604,10 +730,12 @@
         copy.wait()
 
 
-def correct_kernel(vv_hbm, d_ref, o_hbm, vb, g75, g25, in_sem, out_sem):
+def correct_kernel(vv_hbm, d_ref, o_hbm, vb, refined, in_sem, out_sem):
     sub, lane = iotas()
     lanes = vb.shape[-1]
     half = lanes // 256
+    up_index = (sub // 4) * 4 + (sub + 1) % 4
+    down_index = (sub // 4) * 4 + (sub + 3) % 4
 
     def load(m):
         return pltpu.make_async_copy(vv_hbm.at[m], vb.at[m], in_sem.at[m])
@@ -627,21 +755,22 @@
             high = 0.75 * tiles[i] + 0.25 * after[i]
             fine = jnp.where(lane % 2 == 0, take(low, index, 1), take(high, index, 1))
             near_part, far_part = 0.75 * fine, 0.25 * fine
-            for h in range(2):
-                near = 4 * h + sub // 2
-                far = 4 * h + (sub // 2 + 3 + 2 * (sub % 2)) % 4
-                value = take(near_part, near, 0) + take(far_part, far, 0)
-                columns = pl.ds(128 * (t + half * h), 128)
-                g75[k, :, columns] = 0.75 * value
-                g25[k, :, columns] = 0.25 * value
+            refined.at[k][pl.ds(16 * t, 8, stride=2), :] = near_part + take(far_part, down_index, 0)
+            refined.at[k][pl.ds(16 * t + 1, 8, stride=2), :] = near_part + take(far_part, up_index, 0)
+
+    def refined_row(k):
+        return jnp.concatenate(
+            [refined[k, pl.ds(16 * t + 8 * h, 8), :] for h in range(2) for t in range(half)], axis=1
+        )
 
     def node(m):
-        each(10, lambda k: spread(m, k), 2)
+        each(10, lambda k: spread(m, k), 5)
         load(m).wait()
 
         def rows(k):
-            vb[m, 2 * k] = vb[m, 2 * k] + g75[k + 1] + g25[k]
-            vb[m, 2 * k + 1] = vb[m, 2 * k + 1] + g75[k + 1] + g25[k + 2]
+            own = 0.75 * refined_row(k + 1)
+            vb[m, 2 * k] = vb[m, 2 * k] + (own + 0.25 * refined_row(k))
+            vb[m, 2 * k + 1] = vb[m, 2 * k + 1] + (own + 0.25 * refined_row(k + 2))
             store(m, 2 * k).start()
             store(m, 2 * k + 1).start()
 
@@ -674,13 +803,13 @@
         in_specs=[anywhere],
         out_specs=(anywhere, anywhere),
         scratch_shapes=[
-            pltpu.VMEM((3, 22, 8, lanes), F32), fine(22), fine(20), fine(20), fine(20), fine(20), fine(20), fine(20), fine(18), fine(16),
+            pltpu.VMEM((3, 22, 8, lanes), F32), fine(22), fine(20), fine(20), fine(20), fine(20), fine(20), fine(20), fine(18), fine(16), pltpu.VMEM((2, ROWS[1][1], 8, lanes), F32), pltpu.VMEM((2, ROWS[1][1], 8, lanes), F32),
             coarse(10), coarse(10), coarse(10), coarse(10), coarse(12), coarse(10),
             tiles(2, GROUP, 2, 5), tiles(GROUP, 2, 5), tiles(2, 5), tiles(2, GROUP, 3, 2, 5), tiles(3, 2, 5),
-            pltpu.VMEM((24, 8, 256), F32), pltpu.VMEM((24, 8, 256), F32), tiles(GROUP, 3, 8), tiles(3, 10, GROUP),
+            pltpu.VMEM((24, 8, 256), F32), pltpu.VMEM((24, 8, 256), F32), tiles(GROUP, 3, 10), tiles(GROUP, 3, 10), tiles(2, GROUP),
             pltpu.VMEM((3, 10, 8, half), F32), pltpu.VMEM((6, lanes // 16, 128), F32),
-            dma(3, 16), dma(2), dma(2), dma(2), dma(2), dma(2, GROUP, 3), dma(2, GROUP, 3), dma(GROUP, 3), dma(3), dma(3),
-            dma(GROUP, 3), dma(GROUP, 3), dma(3), dma(3), dma(2), dma(2), dma(5),
+            dma(3, 16), dma(2), dma(2), dma(2, 4), dma(2, 4), dma(2), dma(2), dma(2, GROUP, 3), dma(2, GROUP, 3), dma(GROUP, 3), dma(3), dma(3),
+            dma(GROUP), dma(GROUP), dma(2), dma(GROUP, 2), dma(5), dma(5), dma(3), dma(2), dma(4), dma(2), dma(2), dma(2), dma(10),
         ],
         compiler_params=pltpu.CompilerParams(
             collective_id=0, has_side_effects=True, vmem_limit_bytes=48 * 1024 * 1024
@@ -693,7 +822,7 @@
         in_specs=[anywhere, pl.BlockSpec(memory_space=pltpu.VMEM)],
         out_specs=anywhere,
         scratch_shapes=[
-            pltpu.VMEM((3, rows, 8, lanes), F32), pltpu.VMEM((10, 8, lanes), F32), pltpu.VMEM((10, 8, lanes), F32),
+            pltpu.VMEM((3, rows, 8, lanes), F32), pltpu.VMEM((10, lanes // 16, 128), F32),
             dma(3), dma(3, 16),
         ],
         compiler_params=pltpu.CompilerParams(vmem_limit_bytes=48 * 1024 * 1024),

time: 61 us -> 54.4 us (0.89); the launches traced: 60.1 us -> 54.4 us
  Pallas kernels: 60.1 us -> 54.4 us
    pallas_call x1, Pallas kernels: 54.7 us -> 49.9 us  [on_device(): pl.pallas_call(main_kernel, name='sweeps', out_shape=(jax.ShapeDtypeStruc...]
    pallas_call x1, Pallas kernels: 5.35 us -> 4.42 us  [on_device(): pl.pallas_call(correct_kernel, name='correct', out_shape=jax.ShapeDtypeSt...]
where the time goes in v3:
time: 54.4 us
  Pallas kernels  54.4 us (100%)
    pallas_call x1, Pallas kernels, on_device(): pl.pallas_call(main_kernel, name='sweeps', out_shape=(jax.ShapeDtypeStruc...  49.9 us
    pallas_call x1, Pallas kernels, on_device(): pl.pallas_call(correct_kernel, name='correct', out_shape=jax.ShapeDtypeSt...  4.42 us

profile of v3, /device:TPU:6, one launch (start us, length us, event | category | flops | bytes accessed | tf_op | source)
XLA Modules:
  0.0 54.4 jit_solution(6186573318380915813)
XLA Ops:
  0.0 49.9 %sweeps.1 = (f32[3,16,8,2048]{3,2,1,0:T(8,128)S(1)}, f32[3,10,8,512]{3,2,1,0:T(8,128)S(1)}) custom-call(f32[1,3,8,16,2048]{4,3,2,1,0:T(8,128)} %u_hbm.1), custom_call_target="tpu_custom_call" | custom-call | tf_op jit(solution)/shard_map/sweeps/pallas_call | solution.py:796
  50.0 4.4 %correct.1 = f32[1,3,8,16,2048]{4,3,2,1,0:T(8,128)} custom-call(f32[3,16,8,2048]{3,2,1,0:T(8,128)S(1)} %get-tuple-element.7.vv_hbm, f32[3,10,8,512]{3,2,1,0:T(8,128)S(1)} %get-tuple-element.8.d_ref), custom_call_target="tpu_custom_call" | custom-call | tf_op jit(solution)/shard_map/correct/pallas_call | solution.py:818

commit v4 on v3

--- a/solution.py
+++ b/solution.py
@@ -188,8 +188,8 @@
 
 def main_kernel(
     u_hbm, vv_hbm, d_hbm,
-    ub, bb, p0, kk, q1, v1, mm, p2, v2, vin, around, relay, c0, c1, c2, c2p, a0, a1, pack, cpack, wpack, rx, wx, w0, w1, res, home, edges, dd, staging,
-    load_sem, u_send, u_recv, e_send, e_recv, h_send, h_recv, a_send, a_recv, c_send, w_send, w_recv, r_send, r_recv, g_send, g_recv, v_send, v_recv, o_send, o_recv, q_send, q_recv,
+    ub, bb, p0, kk, q1, v1, mm, p2, v2, vin, around, relay, c0, c1, c2, c2p, a0, a1, pack, cpack, wpack, rx, wx, w0, w1, res, home, edges, meter, dd, staging,
+    load_sem, u_send, u_recv, e_send, e_recv, h_send, h_recv, a_send, a_recv, w_send, w_recv, r_send, r_recv, g_send, g_recv, v_send, v_recv, o_send, o_recv, q_send, q_recv,
     p_send, p_recv, out_sem,
 ):
     tm, sp = lax.axis_index("tm"), lax.axis_index("space")
@@ -203,23 +203,26 @@
     sides = ((left, 2), (sp, 1), (right, 0))
 
     def load(m, r):
-        return pltpu.make_async_copy(u_hbm.at[0, m, :, r, :], ub.at[m, r + 3], load_sem.at[m, r])
+        return u_hbm.at[0, m, :, r, :], ub.at[m, r + 3]
 
     def remote(src, dst, send, recv, t, s):
         return pltpu.make_async_remote_copy(
             src_ref=src, dst_ref=dst, send_sem=send, recv_sem=recv, device_id=(t, s), device_id_type=MESH
         )
 
+    def all_tiles(count, sem):
+        return remote(meter.at[pl.ds(0, count)], meter.at[pl.ds(0, count)], sem, sem, tm, left)
+
     def edge_row(k):
         return jnp.where(k < 3, k, k + 10)
 
     def load_edges(k):
         for m in range(3):
-            load(m, edge_row(k)).start()
+            pltpu.make_async_copy(*load(m, edge_row(k)), load_sem.at[0]).start()
 
     def load_inner(k):
         for m in range(3):
-            load(m, k + 3).start()
+            pltpu.make_async_copy(*load(m, k + 3), load_sem.at[1]).start()
 
     each(6, load_edges)
     each(10, load_inner)
@@ -252,18 +255,14 @@
     def _():
         pl.semaphore_wait(barrier, 3 * GROUP - 1)
 
-    def wait_edges(k):
-        for m in range(3):
-            load(m, edge_row(k)).wait()
-
-    def wait_inner(k):
-        for m in range(3):
-            load(m, k + 3).wait()
-
-    each(6, wait_edges)
+    def wait_rows(count, sem):
+        rows = ub.at[:, pl.ds(3, count)]
+        pltpu.make_async_copy(rows, rows, sem).wait()
+
+    wait_rows(6, load_sem.at[0])
     u_copies = [
         remote(ub.at[:, pl.ds(18, 1)], ub.at[:, pl.ds(2, 1)], u_send.at[0], u_recv.at[0], tm, right),
-        remote(ub.at[:, pl.ds(3, 1)], ub.at[:, pl.ds(19, 1)], u_send.at[1], u_recv.at[1], tm, left),
+        remote(ub.at[:, pl.ds(3, 1)], ub.at[:, pl.ds(19, 1)], u_send.at[0], u_recv.at[0], tm, left),
     ]
     for copy in u_copies:
         copy.start()
@@ -318,14 +317,14 @@
             for s, p in sides:
                 if p == piece and (d > 0 or p != 1):
                     copy = remote(
-                        cpack.at[keeper], wx.at[p], c_send.at[d, p], w_recv.at[p], team + keeper, s
+                        cpack.at[keeper], wx.at[p], a_send.at[1], w_recv.at[0], team + keeper, s
                     )
                     go(copy)
 
     def terms_copy(block, fields, keeper, slot, m, piece, s):
         return remote(
             pack.at[block, keeper, pl.ds(0, fields)], rx.at[block, m, piece, pl.ds(0, fields)],
-            a_send.at[block, slot, piece], a_recv.at[block, m, piece], team + keeper, s,
+            a_send.at[block], a_recv.at[block], team + keeper, s,
         )
 
     def sized(block, m, go):
@@ -352,19 +351,11 @@
 
         each(GROUP, mate)
 
+    def fields_beside(block, m):
+        return jnp.where(m < 2 + block, 2, jnp.where(m == 2 + block, 1, 0))
+
     def wait_terms(block):
-        def slice_terms(m):
-            @pl.when(m != spot)
-            def _():
-                terms_copy(block, 2, spot, 0, m, 1, left).wait_recv()
-
-            def beside(fields):
-                for piece in (0, 2):
-                    terms_copy(block, fields, spot, 0, m, piece, left).wait_recv()
-
-            sized(block, m, beside)
-
-        each(GROUP, slice_terms)
+        all_tiles(10 * (GROUP - 1) + 10 * (5 + 2 * block), a_recv.at[block]).wait_recv()
 
     def send_terms(block):
         for k in BLOCKS[block]:
@@ -387,12 +378,12 @@
     for n, (field, offset, up, down) in enumerate(((bb, 3, 14, 1), (v1, 2, 14, 1), (mm, 2, 14, 1), (c0, 1, 7, 0))):
         up_target, down_target = up + offset - rows_of[n], down + offset + rows_of[n]
         rim_copies += [
-            remote(field.at[pl.ds(up + offset, 1)], field.at[pl.ds(up_target, 1)], e_send.at[0, n], e_recv.at[0, n], tm, right),
-            remote(field.at[pl.ds(down + offset, 1)], field.at[pl.ds(down_target, 1)], e_send.at[1, n], e_recv.at[1, n], tm, left),
+            remote(field.at[pl.ds(up + offset, 1)], field.at[pl.ds(up_target, 1)], e_send.at[0], e_recv.at[0], tm, right),
+            remote(field.at[pl.ds(down + offset, 1)], field.at[pl.ds(down_target, 1)], e_send.at[0], e_recv.at[0], tm, left),
         ]
     for copy in rim_copies:
         copy.start()
-    each(10, wait_inner)
+    wait_rows(10, load_sem.at[1])
     for k in range(1, 7):
         restrict_first(k)
 
@@ -458,8 +449,7 @@
         c1[i + 1] = restrict_row(v1[2 * i + 2] + v1[2 * i + 3], staging.at[n])
     send_terms(0)
 
-    for copy in u_copies:
-        copy.wait_recv()
+    all_tiles(6 * 16, u_recv.at[0]).wait_recv()
     for r in (-1, 16):
         local_terms(r)
     for r in (0, 15):
@@ -468,8 +458,7 @@
         second_sweep(r)
     for i in (1, 6):
         coarse_row(i)
-    for copy in rim_copies:
-        copy.wait_recv()
+    all_tiles(2 * (3 * 16 + 4), e_recv.at[0]).wait_recv()
     for r in (-1, 16):
         first_sweep(r)
     for r in (-1, 0, 15, 16):
@@ -478,6 +467,11 @@
         coarse_row(i)
     each(2, restrict_rim, 2)
 
+
+    @pl.when(is_first)
+    def _():
+        all_tiles(10 * (3 * GROUP - 1), a_send.at[1]).wait_send()
+
     send_terms(1)
 
     @pl.when(not_last)
@@ -486,14 +480,14 @@
 
 
     c2_up = remote(c2.at[pl.ds(8, 1)], c2.at[pl.ds(0, 1)], h_send.at[0], h_recv.at[0], tm, right)
-    c2_down = remote(c2.at[pl.ds(1, 1)], c2.at[pl.ds(9, 1)], h_send.at[1], h_recv.at[1], tm, left)
+    c2_down = remote(c2.at[pl.ds(1, 1)], c2.at[pl.ds(9, 1)], h_send.at[0], h_recv.at[0], tm, left)
     c2_up.start()
     c2_down.start()
     v1_out = pltpu.make_async_copy(v1.at[pl.ds(2, 16)], vv_hbm.at[1], out_sem.at[0])
     v2_out = pltpu.make_async_copy(v2.at[pl.ds(1, 16)], vv_hbm.at[2], out_sem.at[1])
     u0_out = pltpu.make_async_copy(ub.at[0, pl.ds(3, 16)], vv_hbm.at[0], out_sem.at[2])
     p_next = [
-        remote(c2.at[pl.ds(k, 1)], c2p.at[pl.ds(k, 1)], p_send.at[n], p_recv.at[n], tm + 1, sp) for n, k in enumerate((0, 9))
+        remote(c2.at[pl.ds(k, 1)], c2p.at[pl.ds(k, 1)], p_send.at[0], p_recv.at[0], tm + 1, sp) for n, k in enumerate((0, 9))
     ]
     v1_out.start()
     v2_out.start()
@@ -519,8 +513,7 @@
     def _():
         relay_in[1].start()
 
-    c2_up.wait_recv()
-    c2_down.wait_recv()
+    all_tiles(2 * 4, h_recv.at[0]).wait_recv()
 
     @pl.when(not_last)
     def _():
@@ -531,12 +524,13 @@
     def _():
         start_hop(2)
 
-    for piece in (0, 2):
-        remote(wpack, wx.at[piece], w_send.at[piece], w_recv.at[piece], tm, left).wait_recv()
+    @pl.when(is_first)
+    def _():
+        all_tiles(20, w_recv.at[0]).wait_recv()
 
     @pl.when(not_first)
     def _():
-        remote(wpack, wx.at[1], w_send.at[1], w_recv.at[1], tm, left).wait_recv()
+        all_tiles(30, w_recv.at[0]).wait_recv()
 
     for piece in range(3):
         for r in range(8):
@@ -550,15 +544,15 @@
 
         @pl.when(m != spot)
         def _():
-            go(remote(res.at[m], home.at[spot], r_send.at[m], r_recv.at[spot], owner, sp))
+            go(remote(res.at[m], home.at[spot], r_send.at[0], r_recv.at[0], owner, sp))
 
         @pl.when(m == spot)
         def _():
             here()
 
     end_copies = [
-        remote(res.at[last_m, 2, 8], edges.at[0, spot], g_send.at[0], g_recv.at[spot, 0], team + last_m, right),
-        remote(res.at[last_m, 2, 1], edges.at[1, spot], g_send.at[1], g_recv.at[spot, 1], team + last_m, left),
+        remote(res.at[last_m, 2, 8], edges.at[0, spot], g_send.at[0], g_recv.at[0], team + last_m, right),
+        remote(res.at[last_m, 2, 1], edges.at[1, spot], g_send.at[0], g_recv.at[0], team + last_m, left),
     ]
 
     def sweep(m):
@@ -591,7 +585,7 @@
         copy.start()
 
     group_sends = [
-        remote(wpack, wx.at[piece], w_send.at[piece], w_recv.at[piece], tm + GROUP, s) for s, piece in sides
+        remote(wpack, wx.at[piece], w_send.at[0], w_recv.at[0], tm + GROUP, s) for s, piece in sides
     ]
 
     @pl.when(first_team)
@@ -604,19 +598,13 @@
 
     @pl.when(tm == GROUP - 1)
     def _():
-        for copy in group_sends:
-            copy.wait_send()
+        all_tiles(30, w_send.at[0]).wait_send()
         v_parts[4].start()
 
     @pl.when(first_team)
     def _():
         start_hop(2)
 
-
-    def wait_home(t):
-        @pl.when(t != spot)
-        def _():
-            remote(res.at[0], home.at[t], r_send.at[0], r_recv.at[t], tm, left).wait_recv()
 
     def vin_out(n):
         rows = pl.ds(*ROWS[n])
@@ -631,6 +619,26 @@
             for i in range(first // 2, (first + count) // 2):
                 c2p[i + 1] = restrict_row(vin[2 * i] + vin[2 * i + 1], staging.at[i % 6])
 
+    all_tiles(6 * 16, u_send.at[0]).wait_send()
+    all_tiles(2 * (3 * 16 + 4), e_send.at[0]).wait_send()
+    all_tiles(2 * 4, h_send.at[0]).wait_send()
+    for block in range(2):
+        for fields in range(3):
+            pl.when(fields_beside(block, spot) == fields)(
+                lambda: all_tiles(10 * (GROUP - 1) + 10 * GROUP * fields, a_send.at[block]).wait_send()
+            )
+
+    @pl.when(is_first)
+    def _():
+        u0_out.wait()
+
+    @pl.when(tm < GROUP - 1)
+    def _():
+        all_tiles(30, w_send.at[0]).wait_send()
+
+    v1_out.wait()
+    v2_out.wait()
+
     start_relay(1)
 
     @pl.when(not_first)
@@ -638,7 +646,7 @@
         take_parts((0, 2))
         take_parts((1, 3, 4))
 
-    each(GROUP, wait_home)
+    all_tiles(30 * (GROUP - 1), r_recv.at[0]).wait_recv()
 
     for t in range(GROUP):
         columns = pl.ds(128 * t, 128)
@@ -647,10 +655,10 @@
 
     @pl.when(spot == last_m)
     def _():
+        all_tiles(2 * GROUP, g_recv.at[0]).wait_recv()
         for t in range(GROUP):
             columns = pl.ds(128 * t, 128)
             for side in range(2):
-                remote(res.at[0, 2, 8], edges.at[side, t], g_send.at[side], g_recv.at[t, side], tm, left).wait_recv()
                 dd[2, 9 * side, :, columns] = edges[side, t] - c2[9 * side, :, columns]
 
     d_out = [
@@ -665,37 +673,19 @@
 
     @pl.when(not_first)
     def _():
-        for copy in p_next:
-            copy.wait_recv()
+        all_tiles(8, p_recv.at[0]).wait_recv()
         for t in range(GROUP):
             columns = pl.ds(128 * t, 128)
             dd[0, :, :, columns] = home[t, 0] - c2p[:, :, columns]
 
     d_out[1].start()
 
-    for copy in (*u_copies, *rim_copies, c2_up, c2_down):
-        copy.wait_send()
-    for block in range(2):
-        terms_copies(block, lambda copy: copy.wait_send())
-    each(GROUP, lambda m: go_home(m, lambda copy: copy.wait_send(), lambda: None))
-    for copy in end_copies:
-        copy.wait_send()
-
-    @pl.when(is_first)
-    def _():
-        for piece in range(3):
-            start_copies(piece, lambda copy: copy.wait_send())
-        u0_out.wait()
-
-    @pl.when(tm < GROUP - 1)
-    def _():
-        for copy in group_sends:
-            copy.wait_send()
+    all_tiles(30 * (GROUP - 1), r_send.at[0]).wait_send()
+    all_tiles(2, g_send.at[0]).wait_send()
 
     @pl.when(not_last)
     def _():
-        for copy in p_next:
-            copy.wait_send()
+        all_tiles(8, p_send.at[0]).wait_send()
         for n in (0, 2, 4):
             v_parts[n].wait_send()
 
@@ -724,8 +714,6 @@
         for n in range(5):
             vin_out(n).wait()
 
-    v1_out.wait()
-    v2_out.wait()
     for copy in d_out:
         copy.wait()
 
@@ -741,7 +729,7 @@
         return pltpu.make_async_copy(vv_hbm.at[m], vb.at[m], in_sem.at[m])
 
     def store(m, r):
-        return pltpu.make_async_copy(vb.at[m, r], o_hbm.at[0, m, :, r, :], out_sem.at[m, r])
+        return pltpu.make_async_copy(vb.at[m, r], o_hbm.at[0, m, :, r, :], out_sem)
 
     for m in range(3):
         load(m).start()
@@ -778,11 +766,7 @@
 
     each(3, node)
 
-    def drain(k):
-        for m in range(3):
-            store(m, k).wait()
-
-    each(16, drain)
+    pltpu.make_async_copy(vb, vb, out_sem).wait()
 
 
 def on_device(node_values):
@@ -806,10 +790,10 @@
             pltpu.VMEM((3, 22, 8, lanes), F32), fine(22), fine(20), fine(20), fine(20), fine(20), fine(20), fine(20), fine(18), fine(16), pltpu.VMEM((2, ROWS[1][1], 8, lanes), F32), pltpu.VMEM((2, ROWS[1][1], 8, lanes), F32),
             coarse(10), coarse(10), coarse(10), coarse(10), coarse(12), coarse(10),
             tiles(2, GROUP, 2, 5), tiles(GROUP, 2, 5), tiles(2, 5), tiles(2, GROUP, 3, 2, 5), tiles(3, 2, 5),
-            pltpu.VMEM((24, 8, 256), F32), pltpu.VMEM((24, 8, 256), F32), tiles(GROUP, 3, 10), tiles(GROUP, 3, 10), tiles(2, GROUP),
+            pltpu.VMEM((24, 8, 256), F32), pltpu.VMEM((24, 8, 256), F32), tiles(GROUP, 3, 10), tiles(GROUP, 3, 10), tiles(2, GROUP), tiles(110),
             pltpu.VMEM((3, 10, 8, half), F32), pltpu.VMEM((6, lanes // 16, 128), F32),
-            dma(3, 16), dma(2), dma(2), dma(2, 4), dma(2, 4), dma(2), dma(2), dma(2, GROUP, 3), dma(2, GROUP, 3), dma(GROUP, 3), dma(3), dma(3),
-            dma(GROUP), dma(GROUP), dma(2), dma(GROUP, 2), dma(5), dma(5), dma(3), dma(2), dma(4), dma(2), dma(2), dma(2), dma(10),
+            dma(2), dma(1), dma(1), dma(1), dma(1), dma(1), dma(1), dma(2), dma(2), dma(1), dma(1), dma(1), dma(1),
+            dma(1), dma(1), dma(5), dma(5), dma(3), dma(2), dma(4), dma(2), dma(1), dma(1), dma(10),
         ],
         compiler_params=pltpu.CompilerParams(
             collective_id=0, has_side_effects=True, vmem_limit_bytes=48 * 1024 * 1024
@@ -823,7 +807,7 @@
         out_specs=anywhere,
         scratch_shapes=[
             pltpu.VMEM((3, rows, 8, lanes), F32), pltpu.VMEM((10, lanes // 16, 128), F32),
-            dma(3), dma(3, 16),
+            dma(3), pltpu.SemaphoreType.DMA,
         ],
         compiler_params=pltpu.CompilerParams(vmem_limit_bytes=48 * 1024 * 1024),
     )(vv, dd)

time: 54.4 us -> 52.4 us (0.963)
  Pallas kernels: 54.4 us -> 52.3 us
    pallas_call x1, Pallas kernels: 49.9 us -> 48.3 us  [on_device(): pl.pallas_call(main_kernel, name='sweeps', out_shape=(jax.ShapeDtypeStruc...]
where the time goes in v4:
time: 52.4 us; the launch traced here: 52.3 us
  Pallas kernels  52.3 us (100%)
    pallas_call x1, Pallas kernels, on_device(): pl.pallas_call(main_kernel, name='sweeps', out_shape=(jax.ShapeDtypeStruc...  48.3 us
    pallas_call x1, Pallas kernels, on_device(): pl.pallas_call(correct_kernel, name='correct', out_shape=jax.ShapeDtypeSt...  4 us

profile of v4, /device:TPU:6, one launch (start us, length us, event | category | flops | bytes accessed | tf_op | source)
XLA Modules:
  0.0 52.3 jit_solution(7288924628385317043)
XLA Ops:
  0.0 48.3 %sweeps.1 = (f32[3,16,8,2048]{3,2,1,0:T(8,128)S(1)}, f32[3,10,8,512]{3,2,1,0:T(8,128)S(1)}) custom-call(f32[1,3,8,16,2048]{4,3,2,1,0:T(8,128)} %u_hbm.1), custom_call_target="tpu_custom_call" | custom-call | tf_op jit(solution)/shard_map/sweeps/pallas_call | solution.py:780
  48.3 4.0 %correct.1 = f32[1,3,8,16,2048]{4,3,2,1,0:T(8,128)} custom-call(f32[3,16,8,2048]{3,2,1,0:T(8,128)S(1)} %get-tuple-element.7.vv_hbm, f32[3,10,8,512]{3,2,1,0:T(8,128)S(1)} %get-tuple-element.8.d_ref), custom_call_target="tpu_custom_call" | custom-call | tf_op jit(solution)/shard_map/correct/pallas_call | solution.py:802

commit v5 on v4

--- a/solution.py
+++ b/solution.py
@@ -734,17 +734,34 @@
     for m in range(3):
         load(m).start()
 
-    def spread(m, k):
-        tiles = split_tiles(d_ref[m, k])
-        before, after = lane_neighbours(tiles, lane)
-        for t in range(half):
-            i, index = t // 2, (t % 2) * 64 + lane // 2
-            low = 0.75 * tiles[i] + 0.25 * before[i]
-            high = 0.75 * tiles[i] + 0.25 * after[i]
-            fine = jnp.where(lane % 2 == 0, take(low, index, 1), take(high, index, 1))
-            near_part, far_part = 0.75 * fine, 0.25 * fine
-            refined.at[k][pl.ds(16 * t, 8, stride=2), :] = near_part + take(far_part, down_index, 0)
-            refined.at[k][pl.ds(16 * t + 1, 8, stride=2), :] = near_part + take(far_part, up_index, 0)
+    def spread_lanes(m, t):
+        rows = [split_tiles(d_ref[m, k]) for k in range(10)]
+        wide = jnp.concatenate(
+            [jnp.concatenate([v[t], strip_of(v, t, lane)], axis=1) for v in rows], axis=0
+        )
+        total = None
+        for _ in range(3):
+            part = wide.astype(jnp.bfloat16)
+            wide = wide - part.astype(F32)
+            product = jnp.dot(part, weights, preferred_element_type=F32)
+            total = product if total is None else total + product
+        return total
+
+    row_index = lax.broadcasted_iota(jnp.int32, (256, 256), 0)
+    fine_index = lax.broadcasted_iota(jnp.int32, (256, 256), 1)
+    near = fine_index // 2
+    far = lax.rem(near + 255 + 2 * (fine_index % 2), 256)
+    weights = jnp.where(row_index == near, 0.75, jnp.where(row_index == far, 0.25, 0.0)).astype(jnp.bfloat16)
+
+    def spread_all(m):
+        for i in range(half // 2):
+            refined_lanes = spread_lanes(m, i)
+            for k in range(10):
+                for t in (2 * i, 2 * i + 1):
+                    fine = refined_lanes[8 * k : 8 * k + 8, 128 * (t - 2 * i) : 128 * (t - 2 * i) + 128]
+                    near_part, far_part = 0.75 * fine, 0.25 * fine
+                    refined.at[k][pl.ds(16 * t, 8, stride=2), :] = near_part + take(far_part, down_index, 0)
+                    refined.at[k][pl.ds(16 * t + 1, 8, stride=2), :] = near_part + take(far_part, up_index, 0)
 
     def refined_row(k):
         return jnp.concatenate(
@@ -752,7 +769,7 @@
         )
 
     def node(m):
-        each(10, lambda k: spread(m, k), 5)
+        spread_all(m)
         load(m).wait()
 
         def rows(k):

time: 52.4 us -> 51.4 us (0.981)
  Pallas kernels: 52.3 us -> 51.2 us
    pallas_call x1, Pallas kernels: 4 us -> 2.96 us  [on_device(): pl.pallas_call(correct_kernel, name='correct', out_shape=jax.ShapeDtypeSt...]
where the time goes in v5:
time: 51.4 us; the launch traced here: 51.3 us
  Pallas kernels  51.2 us (100%)
    pallas_call x1, Pallas kernels, on_device(): pl.pallas_call(main_kernel, name='sweeps', out_shape=(jax.ShapeDtypeStruc...  48.3 us
    pallas_call x1, Pallas kernels, on_device(): pl.pallas_call(correct_kernel, name='correct', out_shape=jax.ShapeDtypeSt...  2.96 us

profile of v5, /device:TPU:6, one launch (start us, length us, event | category | flops | bytes accessed | tf_op | source)
XLA Modules:
  0.0 51.3 jit_solution(13547332449260698880)
XLA Ops:
  0.0 48.3 %sweeps.1 = (f32[3,16,8,2048]{3,2,1,0:T(8,128)S(1)}, f32[3,10,8,512]{3,2,1,0:T(8,128)S(1)}) custom-call(f32[1,3,8,16,2048]{4,3,2,1,0:T(8,128)} %u_hbm.1), custom_call_target="tpu_custom_call" | custom-call | tf_op jit(solution)/shard_map/sweeps/pallas_call | solution.py:797
  48.3 3.0 %correct.1 = f32[1,3,8,16,2048]{4,3,2,1,0:T(8,128)} custom-call(f32[3,16,8,2048]{3,2,1,0:T(8,128)S(1)} %get-tuple-element.7.vv_hbm, f32[3,10,8,512]{3,2,1,0:T(8,128)S(1)} %get-tuple-element.8.d_ref), custom_call_target="tpu_custom_call" | custom-call | tf_op jit(solution)/shard_map/correct/pallas_call | solution.py:819

commit v6 on v5

--- a/solution.py
+++ b/solution.py
@@ -105,14 +105,14 @@
 
 
 def put_block(ref, rows, strips, lane):
-    ref[0] = join_strips(strips, lane)
-    for k in range(4):
-        ref[k + 1] = rows[k]
+    for k, place in enumerate((0, 1, 3, 4)):
+        ref[place] = rows[k]
+    ref[2] = join_strips(strips, lane)
 
 
 def get_row(ref, k):
-    strip = pltpu.roll(ref[0], (128 - 32 * k) % 128, 1)
-    return jnp.concatenate([ref[k + 1], strip], axis=1)
+    strip = pltpu.roll(ref[2], (128 - 32 * k) % 128, 1)
+    return jnp.concatenate([ref[k if k < 2 else k + 1], strip], axis=1)
 
 
 def packed_halves(row, staging):
@@ -321,19 +321,21 @@
                     )
                     go(copy)
 
-    def terms_copy(block, fields, keeper, slot, m, piece, s):
+    def terms_copy(block, fields, keeper, m, piece, s, entries=(0, 5)):
+        where = (pl.ds(0, fields), pl.ds(*entries))
         return remote(
-            pack.at[block, keeper, pl.ds(0, fields)], rx.at[block, m, piece, pl.ds(0, fields)],
+            pack.at[(block, keeper, *where)], rx.at[(block, m, piece, *where)],
             a_send.at[block], a_recv.at[block], team + keeper, s,
         )
 
     def sized(block, m, go):
         if block == 0:
-            pl.when(m < 2)(lambda: go(2))
-            pl.when(m == 2)(lambda: go(1))
+            pl.when(m < 2)(lambda: go(2, False))
+            pl.when(m == 2)(lambda: go(1, True))
         else:
-            pl.when(m < 3)(lambda: go(2))
-            pl.when(m == 3)(lambda: go(1))
+            pl.when(m == 0)(lambda: go(2, False))
+            pl.when((m == 1) | (m == 2))(lambda: go(2, True))
+            pl.when(m == 3)(lambda: go(1, True))
 
     def terms_copies(block, go):
         def mate(d):
@@ -341,21 +343,23 @@
 
             @pl.when(d > 0)
             def _():
-                go(terms_copy(block, 2, keeper, d, spot, 1, sp))
-
-            def beside(fields):
-                go(terms_copy(block, fields, keeper, d, spot, 2, left))
-                go(terms_copy(block, fields, keeper, d, spot, 0, right))
+                go(terms_copy(block, 2, keeper, spot, 1, sp))
+
+            def beside(fields, half):
+                go(terms_copy(block, fields, keeper, spot, 2, left, (0, 3) if half else (0, 5)))
+                go(terms_copy(block, fields, keeper, spot, 0, right, (2, 3) if half else (0, 5)))
 
             sized(block, spot, beside)
 
         each(GROUP, mate)
 
-    def fields_beside(block, m):
-        return jnp.where(m < 2 + block, 2, jnp.where(m == 2 + block, 1, 0))
+    def tiles_beside(block, m):
+        if block == 0:
+            return jnp.where(m < 2, 10, jnp.where(m == 2, 3, 0))
+        return jnp.where(m == 0, 10, jnp.where(m < 3, 6, 3))
 
     def wait_terms(block):
-        all_tiles(10 * (GROUP - 1) + 10 * (5 + 2 * block), a_recv.at[block]).wait_recv()
+        all_tiles(10 * (GROUP - 1) + 2 * (23, 25)[block], a_recv.at[block]).wait_recv()
 
     def send_terms(block):
         for k in BLOCKS[block]:
@@ -623,9 +627,9 @@
     all_tiles(2 * (3 * 16 + 4), e_send.at[0]).wait_send()
     all_tiles(2 * 4, h_send.at[0]).wait_send()
     for block in range(2):
-        for fields in range(3):
-            pl.when(fields_beside(block, spot) == fields)(
-                lambda: all_tiles(10 * (GROUP - 1) + 10 * GROUP * fields, a_send.at[block]).wait_send()
+        for count in (0, 3, 6, 10):
+            pl.when(tiles_beside(block, spot) == count)(
+                lambda: all_tiles(10 * (GROUP - 1) + 2 * GROUP * count, a_send.at[block]).wait_send()
             )
 
     @pl.when(is_first)

time: 51.4 us -> 50.7 us (0.986)
  Pallas kernels: 51.2 us -> 50.5 us
    pallas_call x1, Pallas kernels: 48.3 us -> 47.6 us  [on_device(): pl.pallas_call(main_kernel, name='sweeps', out_shape=(jax.ShapeDtypeStruc...]
where the time goes in v6:
time: 50.7 us; the launch traced here: 50.6 us
  Pallas kernels  50.5 us (100%)
    pallas_call x1, Pallas kernels, on_device(): pl.pallas_call(main_kernel, name='sweeps', out_shape=(jax.ShapeDtypeStruc...  47.6 us
    pallas_call x1, Pallas kernels, on_device(): pl.pallas_call(correct_kernel, name='correct', out_shape=jax.ShapeDtypeSt...  2.96 us

profile of v6, /device:TPU:6, one launch (start us, length us, event | category | flops | bytes accessed | tf_op | source)
XLA Modules:
  0.0 50.6 jit_solution(15485051552570662160)
XLA Ops:
  0.0 47.6 %sweeps.1 = (f32[3,16,8,2048]{3,2,1,0:T(8,128)S(1)}, f32[3,10,8,512]{3,2,1,0:T(8,128)S(1)}) custom-call(f32[1,3,8,16,2048]{4,3,2,1,0:T(8,128)} %u_hbm.1), custom_call_target="tpu_custom_call" | custom-call | tf_op jit(solution)/shard_map/sweeps/pallas_call | solution.py:801
  47.6 3.0 %correct.1 = f32[1,3,8,16,2048]{4,3,2,1,0:T(8,128)} custom-call(f32[3,16,8,2048]{3,2,1,0:T(8,128)S(1)} %get-tuple-element.7.vv_hbm, f32[3,10,8,512]{3,2,1,0:T(8,128)S(1)} %get-tuple-element.8.d_ref), custom_call_target="tpu_custom_call" | custom-call | tf_op jit(solution)/shard_map/correct/pallas_call | solution.py:823

commit v7 on v6

--- a/solution.py
+++ b/solution.py
@@ -188,7 +188,7 @@
 
 def main_kernel(
     u_hbm, vv_hbm, d_hbm,
-    ub, bb, p0, kk, q1, v1, mm, p2, v2, vin, around, relay, c0, c1, c2, c2p, a0, a1, pack, cpack, wpack, rx, wx, w0, w1, res, home, edges, meter, dd, staging,
+    ub, bb, p0, kk, q1, v1, mm, p2, v2, vin, around, relay, c0, c1, c2, c2p, a0, a1, pack, cpack, wpack, rx, wx, w0, w1, res, home, edges, meter, rim, dd, staging,
     load_sem, u_send, u_recv, e_send, e_recv, h_send, h_recv, a_send, a_recv, w_send, w_recv, r_send, r_recv, g_send, g_recv, v_send, v_recv, o_send, o_recv, q_send, q_recv,
     p_send, p_recv, out_sem,
 ):
@@ -291,8 +291,7 @@
         v2[r + 1] = p2[r + 2] + neighbour_sum(mm[r + 1], mm[r + 2], mm[r + 3])
 
     def restrict_rim(k):
-        i = 9 * k - 1
-        c1[i + 1] = restrict_row(v1[2 * i + 2] + v1[2 * i + 3], staging.at[k])
+        c1[9 * k] = rim[k + 2] + restrict_row(v1[17 * k + 1], staging.at[k])
 
     def coarse_row(i):
         r = 2 * i
@@ -376,10 +375,14 @@
     each(6, lambda k: local_terms(edge_row(k)), 3)
     for k in (0, 7):
         restrict_first(k)
-    for r in (1, 14):
+    for n, r in enumerate((14, 1)):
         first_sweep(r)
-    rim_copies, rows_of = [], (16, 16, 16, 8)
-    for n, (field, offset, up, down) in enumerate(((bb, 3, 14, 1), (v1, 2, 14, 1), (mm, 2, 14, 1), (c0, 1, 7, 0))):
+        rim[n] = restrict_row(v1[r + 2], staging.at[n])
+    rim_copies, rows_of = [
+        remote(rim.at[pl.ds(0, 1)], rim.at[pl.ds(2, 1)], e_send.at[0], e_recv.at[0], tm, right),
+        remote(rim.at[pl.ds(1, 1)], rim.at[pl.ds(3, 1)], e_send.at[0], e_recv.at[0], tm, left),
+    ], (16, 16, 8)
+    for n, (field, offset, up, down) in enumerate(((bb, 3, 14, 1), (mm, 2, 14, 1), (c0, 1, 7, 0))):
         up_target, down_target = up + offset - rows_of[n], down + offset + rows_of[n]
         rim_copies += [
             remote(field.at[pl.ds(up + offset, 1)], field.at[pl.ds(up_target, 1)], e_send.at[0], e_recv.at[0], tm, right),
@@ -462,7 +465,7 @@
         second_sweep(r)
     for i in (1, 6):
         coarse_row(i)
-    all_tiles(2 * (3 * 16 + 4), e_recv.at[0]).wait_recv()
+    all_tiles(2 * (2 * 16 + 2 * 4), e_recv.at[0]).wait_recv()
     for r in (-1, 16):
         first_sweep(r)
     for r in (-1, 0, 15, 16):
@@ -624,7 +627,7 @@
                 c2p[i + 1] = restrict_row(vin[2 * i] + vin[2 * i + 1], staging.at[i % 6])
 
     all_tiles(6 * 16, u_send.at[0]).wait_send()
-    all_tiles(2 * (3 * 16 + 4), e_send.at[0]).wait_send()
+    all_tiles(2 * (2 * 16 + 2 * 4), e_send.at[0]).wait_send()
     all_tiles(2 * 4, h_send.at[0]).wait_send()
     for block in range(2):
         for count in (0, 3, 6, 10):
@@ -811,7 +814,7 @@
             pltpu.VMEM((3, 22, 8, lanes), F32), fine(22), fine(20), fine(20), fine(20), fine(20), fine(20), fine(20), fine(18), fine(16), pltpu.VMEM((2, ROWS[1][1], 8, lanes), F32), pltpu.VMEM((2, ROWS[1][1], 8, lanes), F32),
             coarse(10), coarse(10), coarse(10), coarse(10), coarse(12), coarse(10),
             tiles(2, GROUP, 2, 5), tiles(GROUP, 2, 5), tiles(2, 5), tiles(2, GROUP, 3, 2, 5), tiles(3, 2, 5),
-            pltpu.VMEM((24, 8, 256), F32), pltpu.VMEM((24, 8, 256), F32), tiles(GROUP, 3, 10), tiles(GROUP, 3, 10), tiles(2, GROUP), tiles(110),
+            pltpu.VMEM((24, 8, 256), F32), pltpu.VMEM((24, 8, 256), F32), tiles(GROUP, 3, 10), tiles(GROUP, 3, 10), tiles(2, GROUP), tiles(110), coarse(4),
             pltpu.VMEM((3, 10, 8, half), F32), pltpu.VMEM((6, lanes // 16, 128), F32),
             dma(2), dma(1), dma(1), dma(1), dma(1), dma(1), dma(1), dma(2), dma(2), dma(1), dma(1), dma(1), dma(1),
             dma(1), dma(1), dma(5), dma(5), dma(3), dma(2), dma(4), dma(2), dma(1), dma(1), dma(10),

time: 50.7 us -> 50.7 us (level)
  no operation moved by 1% of the time
where the time goes in v7:
time: 50.7 us; the launch traced here: 50.6 us
  Pallas kernels  50.6 us (100%)
    pallas_call x1, Pallas kernels, on_device(): pl.pallas_call(main_kernel, name='sweeps', out_shape=(jax.ShapeDtypeStruc...  47.7 us
    pallas_call x1, Pallas kernels, on_device(): pl.pallas_call(correct_kernel, name='correct', out_shape=jax.ShapeDtypeSt...  2.96 us

profile of v7, /device:TPU:6, one launch (start us, length us, event | category | flops | bytes accessed | tf_op | source)
XLA Modules:
  0.0 50.6 jit_solution(9439893237582221801)
XLA Ops:
  0.0 47.7 %sweeps.1 = (f32[3,16,8,2048]{3,2,1,0:T(8,128)S(1)}, f32[3,10,8,512]{3,2,1,0:T(8,128)S(1)}) custom-call(f32[1,3,8,16,2048]{4,3,2,1,0:T(8,128)} %u_hbm.1), custom_call_target="tpu_custom_call" | custom-call | tf_op jit(solution)/shard_map/sweeps/pallas_call | solution.py:804
  47.7 3.0 %correct.1 = f32[1,3,8,16,2048]{4,3,2,1,0:T(8,128)} custom-call(f32[3,16,8,2048]{3,2,1,0:T(8,128)S(1)} %get-tuple-element.7.vv_hbm, f32[3,10,8,512]{3,2,1,0:T(8,128)S(1)} %get-tuple-element.8.d_ref), custom_call_target="tpu_custom_call" | custom-call | tf_op jit(solution)/shard_map/correct/pallas_call | solution.py:826
